TPU v7x, 128 devices: a whole 4x4x4 slice. The times are simulated.
128 devices in a mesh: row: 8 (over x, core), seq: 16 (over z, y).
Axes of the slice: x: 4, y: 4, z: 4, core: 2. Of those that a mesh axis runs over, the one named last changes fastest.
Arguments:
- tokens: bfloat16 [8, 2304, 512], P('row', 'seq'), may hold values from -6 to 6
- segment: int32 [8, 2304], P('row', 'seq'), may hold values from 0 to 2303, as said below
- w_qkv: bfloat16 [2, 512, 1536], replicated, may hold values from -0.25 to 0.25
- w_out: bfloat16 [2, 512, 512], replicated, may hold values from -1 to 1
- w_up: bfloat16 [2, 512, 2048], replicated, may hold values from -0.25 to 0.25
- w_down: bfloat16 [2, 2048, 512], replicated, may hold values from -0.125 to 0.125
- gains: bfloat16 [2, 2, 512], replicated, may hold values from 0.5 to 1.5
- cotangent: bfloat16 [8, 2304, 512], P('row', 'seq'), may hold values from -6 to 6
Outputs:
- output: bfloat16 [8, 2304, 512], P('row', 'seq')
- tokens_grad: float32 [8, 2304, 512], P('row', 'seq')
- w_qkv_grad: float32 [2, 512, 1536], replicated
- w_out_grad: float32 [2, 512, 512], replicated
- w_up_grad: float32 [2, 512, 2048], replicated
- w_down_grad: float32 [2, 2048, 512], replicated
- gains_grad: float32 [2, 2, 512], replicated
Inputs may be any that keep to these rules, and one draw needn't show every extreme that they name: `segment`: along a row the document numbers never fall, so each document is a contiguous run of bytes; in one row drawn from the seed a document starts within the first 72 bytes and ends within the last 72.
All inputs are finite; a program needn't handle non-finite values.
Results may differ from a plain program's by a relative error of at most 0.017.
Values may be sent and summed in bfloat16 or wider, within the bound.
A program may use at most 192 MiB of HBM per device.

v0:
```python
import jax
import jax.numpy as jnp
from jax import lax
from jax.sharding import PartitionSpec as P

HEAD = 64


def from_behind(block, axis, distance):
    devices = range(lax.axis_size(axis))
    route = [(i - distance, i) for i in devices if i - distance in devices]
    return lax.ppermute(block, axis, route)


def layer_norm(values, gain):
    center = values - jnp.mean(values, -1, keepdims=True)
    spread = jnp.mean(center * center, -1, keepdims=True)
    return center * lax.rsqrt(spread + 1e-05) * gain


def rotate(tensor, positions, sign):
    row_count, length, width = tensor.shape
    split = tensor.reshape(row_count, length, width // HEAD, HEAD)
    half = HEAD // 2
    freq = 10000.0 ** (-jnp.arange(half, dtype=jnp.float32) / half)
    angle = positions.astype(jnp.float32)[:, None] * freq[None, :]
    cosine = jnp.cos(angle)[None, :, None, :]
    sine = jnp.sin(angle)[None, :, None, :]
    first = split[..., :half]
    second = split[..., half:]
    joined = jnp.concatenate(
        [first * cosine - sign * second * sine, sign * first * sine + second * cosine], -1
    )
    return joined.reshape(row_count, length, width)


def gelu_tanh(values):
    return jax.nn.gelu(values, approximate=True)


def probabilities(query, keys, segment, key_segment, positions):
    row_count, stretch_len, width = query.shape
    key_len = keys.shape[1]
    heads = width // HEAD
    raw = jnp.einsum(
        "rqhe,rkhe->rhqk",
        query.reshape(row_count, stretch_len, heads, HEAD),
        keys.reshape(row_count, key_len, heads, HEAD),
        preferred_element_type=jnp.float32,
    )
    causal = jnp.arange(key_len, dtype=jnp.int32)[None, :] <= positions[:, None]
    allowed = causal[None, None] & (key_segment[:, None, None, :] == segment[:, None, :, None])
    score = jnp.where(allowed, HEAD ** (-0.5) * raw, -1000000000.0)
    top = jnp.max(score, -1, keepdims=True)
    expo = jnp.exp(score - top)
    return expo / jnp.sum(expo, -1, keepdims=True)


def attend_mix(query, keys, values_all, segment, key_segment, positions):
    row_count, stretch_len, width = query.shape
    key_len = keys.shape[1]
    heads = width // HEAD
    prob = probabilities(query, keys, segment, key_segment, positions)
    mixed = jnp.einsum(
        "rhqk,rkhe->rqhe",
        prob.astype(jnp.bfloat16),
        values_all.reshape(row_count, key_len, heads, HEAD),
        preferred_element_type=jnp.float32,
    )
    return mixed.reshape(row_count, stretch_len, width).astype(jnp.bfloat16)


def attention_grads(query, keys, values_all, segment, key_segment, positions, grad_mixed):
    row_count, stretch_len, width = query.shape
    key_len = keys.shape[1]
    heads = width // HEAD
    prob = probabilities(query, keys, segment, key_segment, positions)
    prob_low = prob.astype(jnp.bfloat16)
    mixed_heads = grad_mixed.reshape(row_count, stretch_len, heads, HEAD)
    grad_prob = jnp.einsum(
        "rqhe,rkhe->rhqk",
        mixed_heads,
        values_all.reshape(row_count, key_len, heads, HEAD),
        preferred_element_type=jnp.float32,
    )
    inner = jnp.sum(prob * grad_prob, -1, keepdims=True)
    grad_raw = (HEAD ** (-0.5) * (prob * (grad_prob - inner))).astype(jnp.bfloat16)
    grad_query = jnp.einsum(
        "rhqk,rkhe->rqhe",
        grad_raw,
        keys.reshape(row_count, key_len, heads, HEAD),
        preferred_element_type=jnp.float32,
    )
    grad_keys = jnp.einsum(
        "rhqk,rqhe->rkhe",
        grad_raw,
        query.reshape(row_count, stretch_len, heads, HEAD),
        preferred_element_type=jnp.float32,
    )
    grad_values = jnp.einsum(
        "rhqk,rqhe->rkhe", prob_low, mixed_heads, preferred_element_type=jnp.float32
    )
    return (
        grad_query.reshape(row_count, stretch_len, width),
        grad_keys.reshape(row_count, key_len, width),
        grad_values.reshape(row_count, key_len, width),
    )


def block_forward(
    values, segment, positions, qkv_weight, out_weight, up_weight, down_weight, gain_pair
):
    row_count, stretch_len, width = values.shape
    normed = layer_norm(values, gain_pair[0].astype(jnp.float32)).astype(jnp.bfloat16)
    proj = jnp.einsum("rcd,de->rce", normed, qkv_weight, preferred_element_type=jnp.float32)
    query = rotate(proj[..., :width], positions, 1.0).astype(jnp.bfloat16)
    key_part = rotate(proj[..., width : 2 * width], positions, 1.0).astype(jnp.bfloat16)
    value_part = proj[..., 2 * width :].astype(jnp.bfloat16)
    keys, values_all, key_segment = (
        lax.all_gather(key_part, "seq", axis=1, tiled=True),
        lax.all_gather(value_part, "seq", axis=1, tiled=True),
        lax.all_gather(segment, "seq", axis=1, tiled=True),
    )
    mixed = attend_mix(query, keys, values_all, segment, key_segment, positions)
    attention = (query, keys, values_all, segment, key_segment, positions)
    first = values + jnp.einsum(
        "rcd,de->rce", mixed, out_weight, preferred_element_type=jnp.float32
    )
    normed_two = layer_norm(first, gain_pair[1].astype(jnp.float32)).astype(jnp.bfloat16)
    hidden = jnp.einsum("rcd,df->rcf", normed_two, up_weight, preferred_element_type=jnp.float32)
    active = gelu_tanh(hidden).astype(jnp.bfloat16)
    result = first + jnp.einsum(
        "rcf,fd->rcd", active, down_weight, preferred_element_type=jnp.float32
    )
    stored = (values, normed, attention, positions, mixed, first, normed_two, hidden, active)
    return (stored, result)


def block_backward(stored, gradient, qkv_weight, out_weight, up_weight, down_weight, gain_pair):
    values, normed, attention, positions, mixed, first, normed_two, hidden, active = stored
    grad_low = gradient.astype(jnp.bfloat16)
    down_grad = jnp.einsum("rcf,rcd->fd", active, grad_low, preferred_element_type=jnp.float32)
    grad_active = jnp.einsum(
        "rcd,fd->rcf", grad_low, down_weight, preferred_element_type=jnp.float32
    )
    gelu_pull = jax.vjp(gelu_tanh, hidden)[1]
    grad_hidden = gelu_pull(grad_active)[0].astype(jnp.bfloat16)
    up_grad = jnp.einsum("rcd,rcf->df", normed_two, grad_hidden, preferred_element_type=jnp.float32)
    grad_normed_two = jnp.einsum(
        "rcf,df->rcd", grad_hidden, up_weight, preferred_element_type=jnp.float32
    )
    norm_pull = jax.vjp(layer_norm, first, gain_pair[1].astype(jnp.float32))[1]
    grad_first_norm, gain_two_grad = norm_pull(grad_normed_two)
    grad_first = gradient + grad_first_norm
    grad_first_low = grad_first.astype(jnp.bfloat16)
    out_grad = jnp.einsum("rcd,rce->de", mixed, grad_first_low, preferred_element_type=jnp.float32)
    grad_mixed = jnp.einsum(
        "rce,de->rcd", grad_first_low, out_weight, preferred_element_type=jnp.float32
    ).astype(jnp.bfloat16)
    query, keys, values_all, segment, key_segment, key_positions = attention
    grad_query, grad_keys, grad_values = attention_grads(
        query, keys, values_all, segment, key_segment, key_positions, grad_mixed
    )
    own_keys, own_values = (
        lax.psum_scatter(
            grad_keys.astype(jnp.bfloat16), "seq", scatter_dimension=1, tiled=True
        ).astype(jnp.float32),
        lax.psum_scatter(
            grad_values.astype(jnp.bfloat16), "seq", scatter_dimension=1, tiled=True
        ).astype(jnp.float32),
    )
    grad_proj = jnp.concatenate(
        [rotate(grad_query, positions, -1.0), rotate(own_keys, positions, -1.0), own_values], -1
    ).astype(jnp.bfloat16)
    qkv_grad = jnp.einsum("rcd,rce->de", normed, grad_proj, preferred_element_type=jnp.float32)
    grad_normed = jnp.einsum(
        "rce,de->rcd", grad_proj, qkv_weight, preferred_element_type=jnp.float32
    )
    first_pull = jax.vjp(layer_norm, values, gain_pair[0].astype(jnp.float32))[1]
    grad_values_norm, gain_one_grad = first_pull(grad_normed)
    grad_input = grad_first + grad_values_norm
    gain_grads = jnp.stack([gain_one_grad, gain_two_grad])
    return (grad_input, (qkv_grad, out_grad, up_grad, down_grad, gain_grads))


def per_device(tokens, segment, w_qkv, w_out, w_up, w_down, gains, cotangent):
    row_count, stretch_len, width = tokens.shape
    short_len = stretch_len // 3
    place = lax.axis_index("seq")
    full_pos = place * stretch_len + jnp.arange(stretch_len, dtype=jnp.int32)
    short_pos = place * short_len + jnp.arange(short_len, dtype=jnp.int32)
    inputs = tokens.astype(jnp.float32)
    full_stored, second = block_forward(
        inputs, segment, full_pos, w_qkv[0], w_out[0], w_up[0], w_down[0], gains[0]
    )
    carried = from_behind(second[:, stretch_len - 2 :], "seq", 1)
    shifted = jnp.concatenate([carried, second[:, : stretch_len - 2]], 1)
    pooled = jnp.mean(shifted.reshape(row_count, short_len, 3, width), 2)
    short_segment = segment[:, ::3]
    short_stored, short_out = block_forward(
        pooled, short_segment, short_pos, w_qkv[1], w_out[1], w_up[1], w_down[1], gains[1]
    )
    output = second + jnp.repeat(short_out, 3, axis=1)
    grad_out = cotangent.astype(jnp.float32)
    grad_short = jnp.sum(grad_out.reshape(row_count, short_len, 3, width), 2)
    grad_pooled, short_grads = block_backward(
        short_stored, grad_short, w_qkv[1], w_out[1], w_up[1], w_down[1], gains[1]
    )
    share = grad_pooled / 3.0
    following = from_behind(share[:, :1], "seq", -1)
    spread = jnp.repeat(jnp.concatenate([share, following], 1), 3, axis=1)[:, 2 : stretch_len + 2]
    grad_second = grad_out + spread
    grad_input, full_grads = block_backward(
        full_stored, grad_second, w_qkv[0], w_out[0], w_up[0], w_down[0], gains[0]
    )
    totals = lax.psum(
        (
            full_grads[0],
            full_grads[1],
            full_grads[2],
            full_grads[3],
            full_grads[4],
            short_grads[0],
            short_grads[1],
            short_grads[2],
            short_grads[3],
            short_grads[4],
        ),
        ("row", "seq"),
    )
    qkv_total = jnp.stack([totals[0], totals[5]])
    out_total = jnp.stack([totals[1], totals[6]])
    up_total = jnp.stack([totals[2], totals[7]])
    down_total = jnp.stack([totals[3], totals[8]])
    gain_total = jnp.stack([totals[4], totals[9]])
    return (
        output.astype(jnp.bfloat16),
        grad_input,
        qkv_total,
        out_total,
        up_total,
        down_total,
        gain_total,
    )


def solution(mesh):
    return jax.shard_map(
        per_device,
        mesh=mesh,
        in_specs=(
            P("row", "seq", None),
            P("row", "seq"),
            P(),
            P(),
            P(),
            P(),
            P(),
            P("row", "seq", None),
        ),
        out_specs=(P("row", "seq", None), P("row", "seq", None), P(), P(), P(), P(), P()),
        check_vma=False,
    )
```

profile of v0, /device:TPU:1, one launch (start us, length us, event | category | flops | bytes accessed | tf_op | source)
XLA Modules:
  0.0 832.3 jit_solution(6726428535604540203)
XLA Ops:
  19.2 62.9 %all-reduce.2 = (s32[2304]{0:T(1024)S(1)}, s32[768]{0:T(1024)S(1)}) all-reduce(s32[2304]{0:T(1024)S(1)} %dynamic-update-slice, s32[768]{0:T(1024)S(1)} %bitcast_dynamic-update-slice_fusion), channel_id=1, replica_groups=mesh['row'=8,'seq'=16] {'seq'}, use_global_device_ids=true, to_apply=%add | all-reduce | flops 3072 | bytes 24576
  83.3 2.9 copy.60
  86.3 6.4 fusion.197
  92.7 19.4 %all-gather.3.cloned.1.call-done = bf16[1,2304,512]{2,1,0:T(8,128)(2,1)} async-done(((bf16[1,144,512]{2,1,0:T(8,128)(2,1)}), bf16[1,2304,512]{2,1,0:T(8,128)(2,1)}) %all-gather.3.cloned.1.call-update) | async-done | bytes 2359312 | tf_op jit(solution)/shard_map/all_gather | solution.py:121
  112.1 2.9 copy.54
  115.0 5.8 fusion.70
  125.9 2.9 collective-permute-start
  137.4 23.1 %all_gather.29 = bf16[1,768,512]{2,1,0:T(8,128)(2,1)} all-gather(bf16[1,48,512]{2,1,0:T(8,128)(2,1)S(1)} %convert_element_type.302), channel_id=1, replica_groups=mesh['row'=8,'seq'=16] {'seq'}, dimensions={1}, use_global_device_ids=true | all-gather | bytes 835584 | tf_op jit(solution)/shard_map/all_gather | solution.py:120
  162.8 18.5 %all_gather.26 = bf16[1,768,512]{2,1,0:T(8,128)(2,1)} all-gather(bf16[1,48,512]{2,1,0:T(8,128)(2,1)S(1)} %copy-done.38), channel_id=1, replica_groups=mesh['row'=8,'seq'=16] {'seq'}, dimensions={1}, use_global_device_ids=true | all-gather | bytes 835584 | tf_op jit(solution)/shard_map/all_gather | solution.py:121
  200.0 5.7 convolution_convert_fusion.2
  213.0 4.4 convolution_bitcast_fusion.11
  217.4 73.8 %reduce-scatter.9.cloned.1.call-done = bf16[1,48,512]{2,1,0:T(8,128)(2,1)} async-done(((bf16[1,768,512]{2,1,0:T(8,128)(2,1)}), bf16[1,48,512]{2,1,0:T(8,128)(2,1)}) %reduce-scatter.9.cloned.1.call-update) | async-done | bytes 49168 | tf_op jit(solution)/shard_map/reduce_scatter | solution.py:165
  294.4 71.9 %reduce-scatter.11.cloned.1.call-done = bf16[1,48,512]{2,1,0:T(8,128)(2,1)} async-done(((bf16[1,768,512]{2,1,0:T(8,128)(2,1)}), bf16[1,48,512]{2,1,0:T(8,128)(2,1)}) %reduce-scatter.11.cloned.1.call-update) | async-done | bytes 49168 | tf_op jit(solution)/shard_map/reduce_scatter | solution.py:168
  370.7 2.8 collective-permute-done.1
  375.6 3.2 fusion.79
  383.4 7.6 convolution_convert_fusion
  391.1 11.2 %copy.81 = bf16[1,2304,512]{2,0,1:T(2,128)(2,1)} copy(bf16[1,2304,512]{1,2,0:T(8,128)(2,1)} %bitcast.267) | data formatting | bytes 4718592
  402.3 4.4 copy.120
  406.8 6.4 fusion.201
  413.2 19.4 %fusion.17 = bf16[8,64,2304]{2,1,0:T(8,128)(2,1)S(1)} fusion(f32[8,144,2304]{2,1,0:T(8,128)} %fusion.201, bf16[144,8,32]{0,2,1:T(8,128)(2,1)} %copy-done.44, bf16[144,8,32]{0,2,1:T(8,128)(2,1)} %copy-done.42, f32[8,144,2304]{2,1,0:T(8,128)} %get-tuple-element.78, f32[8,144]{1,0:T(8,128)} %copy-done.96), kind=kOutput, calls=%fused_computation.19 | convolution fusion | flops 359796096 | bytes 23745024 | tf_op jit(solution)/shard_map/rhqk,rqhe->rkhe/dot_general | solution.py:94
  432.6 7.9 copy.79
  440.5 4.4 copy.121
  456.4 2.8 convolution_bitcast_fusion.5
  459.3 2.8 convolution_bitcast_fusion.4
  462.1 18.9 %fusion.67 = f32[1,144,8,64]{1,3,2,0:T(8,128)S(1)} fusion(bf16[2304,8,64]{0,2,1:T(8,128)(2,1)} %bitcast.271, f32[8,144,2304]{2,1,0:T(8,128)} %fusion.201, f32[8,144,2304]{2,1,0:T(8,128)} %get-tuple-element.78, f32[8,144]{1,0:T(8,128)S(1)} %copy-done.97), kind=kOutput, calls=%fused_computation.86 | convolution fusion | flops 358321536 | bytes 23892480 | tf_op jit(solution)/shard_map/rhqk,rkhe->rqhe/dot_general | solution.py:88
  481.0 3.2 reduce-scatter.15.cloned.1.call-done
  485.5 76.1 %reduce-scatter.13.cloned.1.call-done = bf16[144,512]{1,0:T(8,128)(2,1)} async-done(((bf16[2304,512]{1,0:T(8,128)(2,1)}), bf16[144,512]{1,0:T(8,128)(2,1)}) %reduce-scatter.13.cloned.1.call-update) | async-done | bytes 147472
  571.2 67.0 %all-reduce.3 = (f32[1,2,512]{2,1,0:T(2,128)S(1)}, f32[1,2,512]{2,1,0:T(2,128)S(1)}) all-reduce(f32[1,2,512]{2,1,0:T(2,128)S(1)} %maximum_bitcast_fusion.2, f32[1,2,512]{2,1,0:T(2,128)S(1)} %maximum_bitcast_fusion.1), channel_id=1, replica_groups=mesh['row'=8,'seq'=16] {'row','seq'}, use_global_device_ids=true, to_apply=%region_41.42 | all-reduce | flops 2048 | bytes 16384 | tf_op jit(solution)/shard_map/psum | solution.py:216
  639.7 165.3 %all-reduce.7.cloned.1.call-done = (f32[1,512,1536]{2,1,0:T(8,128)}, f32[1,512,1536]{2,1,0:T(8,128)}, f32[1,512,512]{2,1,0:T(8,128)}, f32[1,512,512]{2,1,0:T(8,1...) async-done(((f32[1,512,1536]{2,1,0:T(8,128)}, f32[1,512,1536]{2,1,0:T(8,128)}, ...) | async-done | bytes 25165840 | tf_op jit(solution)/shard_map/psum | solution.py:216
  805.0 6.2 pad_maximum_fusion.2
  814.1 4.8 pad_maximum_fusion
  820.6 4.4 pad_maximum_fusion.1
  (342 shorter events, 95.4 us)
Async XLA Ops:
  7.2 76.2 %all-gather.5.cloned.1.call-start = ((), (), s32[]{:S(2)}) async-start(), calls=%async_computation.5 | async-start | bytes 2506752 | tf_op jit(solution)/shard_map/all_gather | solution.py:120
  11.3 111.4 %copy-start.58 = (f32[1,1,512]{2,1,0:T(1,128)}, f32[1,1,512]{2,1,0:T(1,128)S(1)}, u32[]{:S(2)}) copy-start(f32[1,1,512]{2,1,0:T(1,128)S(1)} %get-tuple-element.68) | copy-start | bytes 6148
  11.3 122.0 %copy-start.63 = (f32[1,1,512]{2,1,0:T(1,128)}, f32[1,1,512]{2,1,0:T(1,128)S(1)}, u32[]{:S(2)}) copy-start(f32[1,1,512]{2,1,0:T(1,128)S(1)} %get-tuple-element.70) | copy-start | bytes 6148
  14.8 71.5 %copy-start.42 = (bf16[144,8,32]{0,2,1:T(8,128)(2,1)}, bf16[144,8,32]{0,2,1:T(8,128)(2,1)S(1)}, u32[]{:S(2)}) copy-start(bf16[144,8,32]{0,2,1:T(8,128)(2,1)S(1)} %get-tuple-element.39) | copy-start | bytes 221188
  14.8 71.5 %copy-start.44 = (bf16[144,8,32]{0,2,1:T(8,128)(2,1)}, bf16[144,8,32]{0,2,1:T(8,128)(2,1)S(1)}, u32[]{:S(2)}) copy-start(bf16[144,8,32]{0,2,1:T(8,128)(2,1)S(1)} %get-tuple-element.40) | copy-start | bytes 221188
  16.0 96.1 %all-gather.3.cloned.1.call-start = ((), (), s32[]{:S(2)}) async-start(), calls=%async_computation.4 | async-start | bytes 2506752 | tf_op jit(solution)/shard_map/all_gather | solution.py:121
  16.8 274.4 %reduce-scatter.9.cloned.1.call-start = ((), (), s32[]{:S(2)}) async-start(), calls=%async_computation.6 | async-start | bytes 835584 | tf_op jit(solution)/shard_map/reduce_scatter | solution.py:165
  82.9 53.4 %copy-start.35 = (f32[48,32]{1,0:T(8,128)}, f32[48,32]{1,0:T(8,128)S(1)}, u32[]{:S(2)}) copy-start(f32[48,32]{1,0:T(8,128)S(1)} %get-tuple-element.76) | copy-start | bytes 18436
  83.3 31.7 %copy-start.32 = (pred[144,2304]{1,0:T(8,128)(4,1)}, pred[144,2304]{1,0:T(8,128)(4,1)S(1)}, u32[]{:S(2)}) copy-start(pred[144,2304]{1,0:T(8,128)(4,1)S(1)} %fusion.65) | copy-start | bytes 995332
  125.9 4.0 collective-permute-start
  129.9 67.1 %copy-start.28 = (f32[48,512]{1,0:T(8,128)}, f32[48,512]{1,0:T(8,128)S(1)}, u32[]{:S(2)}) copy-start(f32[48,512]{1,0:T(8,128)S(1)} %reduce_sum.246) | copy-start | bytes 294916
  136.3 26.5 %copy-start.38 = (bf16[1,48,512]{2,1,0:T(8,128)(2,1)S(1)}, bf16[1,48,512]{2,1,0:T(8,128)(2,1)}, u32[]{:S(2)}) copy-start(bf16[1,48,512]{2,1,0:T(8,128)(2,1)} %slice.328) | copy-start | bytes 147460
  137.1 46.5 %copy-start.47 = (bf16[48,8,32]{2,0,1:T(8,128)(2,1)}, bf16[48,8,32]{2,0,1:T(8,128)(2,1)S(1)}, u32[]{:S(2)}) copy-start(bf16[48,8,32]{2,0,1:T(8,128)(2,1)S(1)} %get-tuple-element.45) | copy-start | bytes 73732
  137.4 46.2 %copy-start.49 = (bf16[48,8,32]{2,0,1:T(8,128)(2,1)S(1)}, bf16[48,8,32]{2,0,1:T(8,128)(2,1)}, u32[]{:S(2)}) copy-start(bf16[48,8,32]{2,0,1:T(8,128)(2,1)} %get-tuple-element.46) | copy-start | bytes 73732
  137.4 46.2 %copy-start.57 = (pred[48,768]{1,0:T(8,128)(4,1)S(1)}, pred[48,768]{1,0:T(8,128)(4,1)}, u32[]{:S(2)}) copy-start(pred[48,768]{1,0:T(8,128)(4,1)} %fusion.137) | copy-start | bytes 110596
  197.1 172.0 %copy-start.16 = (f32[48,512]{1,0:T(8,128)}, f32[48,512]{1,0:T(8,128)S(1)}, u32[]{:S(2)}) copy-start(f32[48,512]{1,0:T(8,128)S(1)} %add_add_fusion.6) | copy-start | bytes 294916
  208.0 158.3 %reduce-scatter.11.cloned.1.call-start = ((), (), s32[]{:S(2)}) async-start(), calls=%async_computation.7 | async-start | bytes 835584 | tf_op jit(solution)/shard_map/reduce_scatter | solution.py:168
  212.9 271.2 %reduce-scatter.15.cloned.1.call-start = ((), (), s32[]{:S(2)}) async-start(), calls=%async_computation.9 | async-start | bytes 2506752
  217.4 148.9 %copy-start.64 = (f32[1,1,512]{2,1,0:T(1,128)S(1)}, f32[1,1,512]{2,1,0:T(1,128)}, u32[]{:S(2)}) copy-start(f32[1,1,512]{2,1,0:T(1,128)} %copy-done.63) | copy-start | bytes 6148
  217.4 148.9 %copy-start.79 = (f32[48]{0:T(128)S(1)}, f32[48]{0:T(128)}, u32[]{:S(2)}) copy-start(f32[48]{0:T(128)} %copy-done.78) | copy-start | bytes 580
  217.4 148.9 %copy-start.84 = (f32[48]{0:T(128)S(1)}, f32[48]{0:T(128)}, u32[]{:S(2)}) copy-start(f32[48]{0:T(128)} %copy-done.83) | copy-start | bytes 580
  292.2 76.7 %copy-start.91 = (f32[48]{0:T(128)S(1)}, f32[48]{0:T(128)}, u32[]{:S(2)}) copy-start(f32[48]{0:T(128)} %copy-done.90) | copy-start | bytes 580
  294.2 81.4 %copy-start.19 = (bf16[1,144,512]{2,1,0:T(8,128)(2,1)S(1)}, bf16[1,144,512]{2,1,0:T(8,128)(2,1)}, u32[]{:S(2)}) copy-start(bf16[1,144,512]{2,1,0:T(8,128)(2,1)} %param.15) | copy-start | bytes 442372
  294.4 81.2 %copy-start.40 = (bf16[48,512]{1,0:T(8,128)(2,1)}, bf16[48,512]{1,0:T(8,128)(2,1)S(1)}, u32[]{:S(2)}) copy-start(bf16[48,512]{1,0:T(8,128)(2,1)S(1)} %concatenate.92) | copy-start | bytes 147460
  369.2 4.3 collective-permute-start.1
  406.7 154.8 %reduce-scatter.13.cloned.1.call-start = ((), (), s32[]{:S(2)}) async-start(), calls=%async_computation.8 | async-start | bytes 2506752
  444.9 360.0 %all-reduce.7.cloned.1.call-start = ((), (), s32[]{:S(2)}) async-start(), calls=%async_computation.10 | async-start | bytes 50331648 | tf_op jit(solution)/shard_map/psum | solution.py:216
  481.0 81.9 %copy-start.34 = (f32[144,32]{0,1:T(8,128)S(1)}, f32[144,32]{0,1:T(8,128)}, u32[]{:S(2)}) copy-start(f32[144,32]{0,1:T(8,128)} %copy-done.33) | copy-start | bytes 55300
  481.0 81.9 %copy-start.46 = (f32[144,32]{0,1:T(8,128)S(1)}, f32[144,32]{0,1:T(8,128)}, u32[]{:S(2)}) copy-start(f32[144,32]{0,1:T(8,128)} %get-tuple-element.71) | copy-start | bytes 55300
  485.4 77.7 %copy-start.51 = (f32[1,1,512]{2,1,0:T(1,128)S(1)}, f32[1,1,512]{2,1,0:T(1,128)}, u32[]{:S(2)}) copy-start(f32[1,1,512]{2,1,0:T(1,128)} %copy-done.50) | copy-start | bytes 6148
  485.5 77.7 %copy-start.54 = (f32[144]{0:T(256)S(1)}, f32[144]{0:T(256)}, u32[]{:S(2)}) copy-start(f32[144]{0:T(256)} %copy-done.53) | copy-start | bytes 1732
  485.5 77.7 %copy-start.56 = (f32[144]{0:T(256)S(1)}, f32[144]{0:T(256)}, u32[]{:S(2)}) copy-start(f32[144]{0:T(256)} %copy-done.55) | copy-start | bytes 1732
  (75 other events, 259.8 us)
Sparse Core Ops, SparseCore 0:
  16.1 48.0 all-gather.4
  67.0 45.0 all-gather.2
  208.1 83.0 reduce-scatter.8
  294.2 71.9 reduce-scatter.10
  406.8 77.2 reduce-scatter.14
  487.3 74.1 reduce-scatter.12
  568.6 236.3 all-reduce.6
where the time goes:
time: 842 us; the launch traced here: 832 us
  waiting for transfers between devices  413 us (49%)
  blocking collectives  172 us (20%)
  matrix products  131 us (16%)
  local copies, waits for them, and re-layouts  63.1 us (7%)
  other arithmetic  31.9 us (4%)
  between operations  17.5 us (2%)
    psum x1, waiting for transfers between devices, per_device(): lax.psum((full_grads[0], full_grads[1], full_grads[2], full_grads[3], ful...  165 us
    unnamed x9, waiting for transfers between devices  79.4 us
    reduce_scatter x1, waiting for transfers between devices, block_backward(): lax.psum_scatter(grad_keys.astype(jnp.bfloat16), 'seq', scatter_dimension...  73.8 us
    reduce_scatter x1, waiting for transfers between devices, block_backward(): lax.psum_scatter(grad_values.astype(jnp.bfloat16), 'seq', scatter_dimensi...  71.9 us
    psum x1, blocking collectives, per_device(): lax.psum((full_grads[0], full_grads[1], full_grads[2], full_grads[3], ful...  67 us
    unnamed x1, blocking collectives  62.9 us
    unnamed x209, local copies, waits for them, and re-layouts  37.5 us
    dot_general x2, matrix products, attention_grads(): jnp.einsum('rhqk,rqhe->rkhe', grad_raw, query.reshape(row_count, stretch_...  25 us
  transfers between devices with their start and end apart: 9, of which 7 were waited for; matrix products, arithmetic and copies ran while one was open for 13% of the time, Pallas kernels for 0%

commit v1 on v0

v1 whole, which is shorter than its diff:
```python
import types

import jax
import jax.numpy as jnp
import numpy as np
from jax import lax
from jax.experimental import pallas as pl
from jax.experimental.pallas import tpu as pltpu
from jax.sharding import PartitionSpec as P

MESH = pl.DeviceIdType.MESH
F32 = jnp.float32
BF16 = jnp.bfloat16

SEQ = 16
LONG = 144
SHORT = 48
D = 512
FF = 2048
GROUPS = 4
NOTE = 16
KV, Q, DM, MIX, DKV, DQ = range(6)
X, Y, Z = range(3)
ORDERS = ((X, Y, Z), (Y, Z, X), (Z, X, Y))


def dot(left, right):
    return jnp.dot(left, right, preferred_element_type=F32)


def dot_nt(left, right):
    return lax.dot_general(left, right, (((1,), (1,)), ((), ())), preferred_element_type=F32)


def dot_tn(left, right):
    return lax.dot_general(left, right, (((0,), (0,)), ((), ())), preferred_element_type=F32)


def lanes(shape):
    return lax.broadcasted_iota(jnp.int32, shape, len(shape) - 1)


def sublanes(shape):
    return lax.broadcasted_iota(jnp.int32, shape, len(shape) - 2)


def normalize(values):
    center = values - jnp.mean(values, -1, keepdims=True)
    scale = lax.rsqrt(jnp.mean(center * center, -1, keepdims=True) + 1e-05)
    return center * scale, scale


def normalize_back(grad, normal, scale, gain):
    inner = grad * gain
    return scale * (
        inner
        - jnp.mean(inner, -1, keepdims=True)
        - normal * jnp.mean(inner * normal, -1, keepdims=True)
    )


def half_turn(tensor):
    up = pltpu.roll(tensor, 96, 1)
    down = pltpu.roll(tensor, 32, 1)
    return jnp.where(lanes(tensor.shape) % 64 < 32, -up, down)


def padded(rows):
    return -(-rows // 32) * 16


def seal(packed):
    rows = packed.shape[0]
    return jnp.concatenate([packed, jnp.zeros((padded(2 * rows) - rows, 128), F32)], 0).astype(BF16)


def pack_pair(pair):
    rows = pair.shape[0] // 2
    top, bottom = pair[:rows], pltpu.roll(pair[rows:], 64, 1)
    low = lanes(top.shape) < 64
    return seal(jnp.where(low, top, bottom)), seal(jnp.where(low, bottom, top))


def unpack_pair(even, odd, rows):
    even, odd = even.astype(F32)[: rows // 2], odd.astype(F32)[: rows // 2]
    low = lanes(even.shape) < 64
    return jnp.concatenate([jnp.where(low, even, odd), pltpu.roll(jnp.where(low, odd, even), 64, 1)], 0)


def unpack_one(packed, rows):
    packed = packed.astype(F32)[: rows // 2]
    return jnp.concatenate([packed, pltpu.roll(packed, 64, 1)], 0).astype(BF16)


def spill(ref, first, values):
    for group in range(GROUPS):
        ref[group, first : first + values.shape[0], :] = values[:, 128 * group : 128 * group + 128]


def every_third(ref, first, group):
    return ref[group, pl.ds(first, SHORT, 3), :]


def remote(src, dst, send, recv, device):
    return pltpu.make_async_remote_copy(
        src_ref=src, dst_ref=dst, send_sem=send, recv_sem=recv, device_id=device, device_id_type=MESH
    )


class Place:
    def __init__(self):
        self.row = lax.axis_index("row")
        self.seq = lax.axis_index("seq")
        self.core = lax.rem(self.row, 2)
        self.at = (self.row // 2, lax.rem(self.seq, 4), self.seq // 4)
        self.head = lax.rem(self.seq, 8)
        self.same = (self.seq // 8 == self.core) & (lax.rem(self.seq, 2) == self.core)
        self.sending, self.coming = [], {}

    def peer(self, axis, distance):
        to = lax.rem(self.at[axis] + distance, 4)
        if axis == X:
            return (to * 2 + self.core, self.seq)
        if axis == Y:
            return (self.row, self.at[Z] * 4 + to)
        return (self.row, to * 4 + self.at[Y])

    def partner(self):
        return (self.row + 1 - 2 * self.core, self.seq)

    def along(self, distance):
        return (self.row, lax.rem(self.seq + distance, SEQ))

    def holder(self, head):
        device = (2 * self.at[X] + lax.rem(self.seq, 2), 8 * self.core + head)
        return device, self.same & (self.head == head)

    def owner(self, index):
        device = (2 * self.at[X] + self.seq // 8, 2 * index + self.core)
        return device, self.same & (self.seq // 2 == index)

    def start(self, copy, key):
        copy.start()
        self.sending.append(copy.wait_send)
        self.coming[key] = copy.wait_recv

    def finish(self, copy, key):
        self.coming.pop(key)
        copy.wait_recv()

    def greet(self, barrier):
        for make in (self.holder, self.owner):
            for index in range(8):
                device, same = make(index)

                @pl.when(jnp.logical_not(same))
                def _():
                    pl.semaphore_signal(barrier, inc=1, device_id=device, device_id_type=MESH)

        others = [self.partner(), self.along(1), self.along(SEQ - 1)]
        others += [self.peer(axis, distance) for axis in (X, Y, Z) for distance in (1, 2, 3)]
        for device in others:
            pl.semaphore_signal(barrier, inc=1, device_id=device, device_id_type=MESH)
        return 16 + len(others) - 2 * self.same.astype(jnp.int32)


class Layer:
    def __init__(self, at, ref, own, index, rows):
        self.at = at
        self.r = ref
        self.s = own
        self.index = index
        self.rows = rows


    def _buffers(self, kind):
        s = self.s
        return (
            (s.kv_out, s.kv_in), (s.q_out, s.q_in), (s.dm_out, s.dm_in),
            (s.mix_out, s.mix_in), (s.dkv_out, s.dkv_in), (s.dq_out, s.dq_in),
        )[kind]

    def _copy(self, kind, index):
        at = self.at
        out, into = self._buffers(kind)
        if kind in (KV, Q, DM):
            (device, same), slot = at.holder(index), at.seq // 2
            target = at.seq if kind == KV else slot
        else:
            (device, same), slot = at.owner(index), at.head
            target = slot
        send, recv = self.s.sems.at[2 * kind, index], self.s.sems.at[2 * kind + 1, slot]
        return out.at[index], into.at[target], send, recv, device, same

    def send(self, kind):
        def one(index, carry):
            src, dst, send, recv, device, same = self._copy(kind, index)

            @pl.when(same)
            def _():
                pltpu.make_async_copy(src, dst, recv).start()

            @pl.when(jnp.logical_not(same))
            def _():
                remote(src, dst, send, recv, device).start()

            return carry

        lax.fori_loop(0, 8, one, 0)
        self.at.sending.append(lambda: self.sent(kind))
        self.at.coming[(self.index, kind)] = lambda: self.receive(kind)

    def _arrival(self, kind, index):
        out, into = self._buffers(kind)
        device, _ = self.at.owner(0)
        sems = self.s.sems
        return remote(out.at[0], into.at[0], sems.at[2 * kind, 0], sems.at[2 * kind + 1, index], device)

    def receive(self, kind):
        self.at.coming.pop((self.index, kind), None)

        def one(index, carry):
            self._arrival(kind, index).wait_recv()
            return carry

        lax.fori_loop(0, 8, one, 0)

    def sent(self, kind):
        def one(index, carry):
            src, dst, send, recv, device, same = self._copy(kind, index)

            @pl.when(jnp.logical_not(same))
            def _():
                remote(src, dst, send, recv, device).wait_send()

            return carry

        lax.fori_loop(0, 8, one, 0)

    def _relay(self, index):
        place = self.s.kv_in.at[2 * index + self.at.core]
        sems = self.s.sems
        return remote(place, place, sems.at[12, index], sems.at[13, index], self.at.partner())

    def receive_keys(self):
        self.at.coming.pop((self.index, KV), None)

        def one(index, carry):
            self._arrival(KV, index).wait_recv()
            self._relay(index).start()
            return carry

        def other(index, carry):
            self._relay(index).wait_recv()
            return carry

        def done(index, carry):
            self._relay(index).wait_send()
            return carry

        lax.fori_loop(0, 8, one, 0)
        lax.fori_loop(0, 8, other, 0)
        self.at.sending.append(lambda: lax.fori_loop(0, 8, done, 0))


    def angles(self):
        table, first = self.r.offsets, self.r.firsts
        place = self.index * SEQ + self.at.seq
        cos_a, sin_a = first[0, pl.ds(place, 1), :], first[1, pl.ds(place, 1), :]
        cos_b, sin_b = table[0, : self.rows, :], table[1, : self.rows, :]
        return cos_a * cos_b - sin_a * sin_b, sin_a * cos_b + cos_a * sin_b

    def gain(self, which):
        return self.r.gains[self.index, which : which + 1, :].astype(F32)

    def project(self, values):
        s, rows = self.s, self.rows
        normal, scale = normalize(values)
        s.normal[0] = normal
        s.scale[0] = jnp.broadcast_to(scale, (rows, 128))
        normed = (normal * self.gain(0)).astype(BF16)
        s.n1[...] = normed
        cosine, sine = self.angles()
        low = lanes((rows, 128)) < 64
        weight = self.r.wqkv.at[self.index]
        for group in range(GROUPS):
            key = dot(normed, weight[:, 512 + 128 * group : 640 + 128 * group])
            value = dot(normed, weight[:, 1024 + 128 * group : 1152 + 128 * group])
            key = key * cosine + half_turn(key) * sine
            value = pltpu.roll(value, 64, 1)
            s.kv_out[2 * group, :rows] = jnp.where(low, key, value).astype(BF16)
            s.kv_out[2 * group + 1, :rows] = jnp.where(low, value, key).astype(BF16)
            query = dot(normed, weight[:, 128 * group : 128 * group + 128])
            query = (query * cosine + half_turn(query) * sine) * 0.125
            s.q_out[2 * group], s.q_out[2 * group + 1] = pack_pair(query)

    def native(self, shape):
        return (lanes(shape) // 64) == lax.rem(self.at.seq, 2)

    def pack_one(self, values):
        rows = self.rows // 2
        return seal(jnp.where(self.native((rows, 128)), values[:rows], pltpu.roll(values[rows:], 64, 1)))

    def split_heads(self):
        s, length = self.s, SEQ * self.rows
        both = s.kv_in[:, : self.rows, :].reshape(length, 128).astype(F32)
        own = self.native((length, 128))
        s.key[...] = jnp.where(own, both, 0.0).astype(BF16)
        s.value[...] = jnp.where(own, pltpu.roll(both, 64, 1), 0.0).astype(BF16)

    def attend(self):
        s, core = self.s, self.at.core
        for index in range(8):
            s.query[index] = unpack_one(s.q_in[index], self.rows)
        if self.index == 0:
            for pair in range(8):
                count = -(-288 * (pair + 1) // 128) * 128
                score = dot_nt(s.query[pair], s.key[:count])
                first = (288 * pair) // 128 * 128
                column = s.column[pair][:, :1]
                allowed = s.line[0:1, :count] == column
                position = sublanes((LONG, count - first)) + (2 * pair + core) * LONG
                causal = lanes((LONG, count - first)) + first <= position
                if first:
                    head = jnp.where(allowed[:, :first], score[:, :first], -1e9)
                    tail = jnp.where(allowed[:, first:] & causal, score[:, first:], -1e9)
                    score = jnp.concatenate([head, tail], 1)
                else:
                    score = jnp.where(allowed & causal, score, -1e9)
                top = jnp.max(score, -1, keepdims=True)
                expo = jnp.exp(score - top)
                prob = (expo * (1.0 / jnp.sum(expo, -1, keepdims=True))).astype(BF16)
                s.prob[pair, :, :count] = prob
                s.mix_out[pair] = self.pack_one(dot(prob, s.value[:count]))
        else:
            count, length = 8 * SHORT, SEQ * SHORT
            score = dot_nt(s.query[...].reshape(count, 128), s.key[...])
            column = s.column[...].reshape(count, 128)[:, :1]
            row = lax.broadcasted_iota(jnp.int32, (8, SHORT, length), 1)
            block = lax.broadcasted_iota(jnp.int32, (8, SHORT, length), 0)
            position = (row + (2 * block + core) * SHORT).reshape(count, length)
            causal = lanes((count, length)) <= position
            score = jnp.where((s.line[0:1, :] == column) & causal, score, -1e9)
            top = jnp.max(score, -1, keepdims=True)
            expo = jnp.exp(score - top)
            prob = (expo * (1.0 / jnp.sum(expo, -1, keepdims=True))).astype(BF16)
            s.prob[...] = prob
            mixed = dot(prob, s.value[...]).reshape(8, SHORT, 128)
            for index in range(8):
                s.mix_out[index] = self.pack_one(mixed[index])

    def feed_forward(self, values):
        i, s = self.index, self.s
        parts = [unpack_pair(s.mix_in[2 * g], s.mix_in[2 * g + 1], self.rows) for g in range(GROUPS)]
        mixed = jnp.concatenate(parts, 1).astype(BF16)
        s.mixed[...] = mixed
        first = values + dot(mixed, self.r.wout[i])
        normal, scale = normalize(first)
        s.normal[1] = normal
        s.scale[1] = jnp.broadcast_to(scale, (self.rows, 128))
        normed = (normal * self.gain(1)).astype(BF16)
        s.n2[...] = normed
        result = first
        for part in range(4):
            at = slice(512 * part, 512 * part + 512)
            hidden = dot(normed, self.r.wup[i, :, at])
            inner = 0.7978845608028654 * (hidden + 0.044715 * hidden * hidden * hidden)
            bend = jnp.tanh(inner)
            active = (0.5 * hidden * (1.0 + bend)).astype(BF16)
            slope = 0.5 * (1.0 + bend) + 0.5 * hidden * (1.0 - bend * bend) * (
                0.7978845608028654 * (1.0 + 3.0 * 0.044715 * hidden * hidden)
            )
            s.slope[:, at] = slope
            s.act[part // 2, :, 512 * (part % 2) : 512 * (part % 2) + 512] = active
            result = result + dot(active, self.r.wdown[i, at, :])
        return result


    def feed_back(self, grad):
        i, s = self.index, self.s
        low = grad.astype(BF16)
        s.glow[...] = low
        back = jnp.zeros((self.rows, D), F32)
        for part in range(4):
            at = slice(512 * part, 512 * part + 512)
            active = dot_nt(low, self.r.wdown[i, at, :])
            hidden = (s.slope[:, at] * active).astype(BF16)
            s.dhid[part // 2, :, 512 * (part % 2) : 512 * (part % 2) + 512] = hidden
            back = back + dot_nt(hidden, self.r.wup[i, :, at])
        normal, scale = s.normal[1], s.scale[1][:, :1]
        self.r.gsum[2 * i + 1 : 2 * i + 2, :] = jnp.sum(back * normal, 0, keepdims=True)
        first = grad + normalize_back(back, normal, scale, self.gain(1))
        s.dfirst[...] = first
        first_low = first.astype(BF16)
        s.dv1[0] = first_low[:, :256]
        s.dv1[1] = first_low[:, 256:]
        for group in range(GROUPS):
            at = slice(128 * group, 128 * group + 128)
            s.dm_out[2 * group], s.dm_out[2 * group + 1] = pack_pair(dot_nt(first_low, self.r.wout[i, at, :]))

    def attend_back(self):
        s, length = self.s, SEQ * self.rows
        own = self.native((length, 128))
        if self.index == 0:
            self.r.dkey[...] = jnp.zeros((length, 128), F32)
            self.r.dvalue[...] = jnp.zeros((length, 128), F32)
            for pair in range(8):
                count = -(-288 * (pair + 1) // 128) * 128
                grad = unpack_one(s.dm_in[pair], self.rows)
                prob = s.prob[pair, :, :count]
                dprob = dot_nt(grad, s.value[:count])
                weighted = prob * dprob
                inner = jnp.sum(weighted, -1, keepdims=True)
                draw = (weighted - prob * inner).astype(BF16)
                s.dq_out[pair] = self.pack_one(dot(draw, s.key[:count]) * 0.125)
                self.r.dkey[:count] += dot_tn(draw, s.query[pair])
                self.r.dvalue[:count] += dot_tn(prob, grad)
            dkey, dvalue = self.r.dkey[...], self.r.dvalue[...]
        else:
            count = 8 * SHORT
            grad = jnp.concatenate([unpack_one(s.dm_in[index], self.rows) for index in range(8)], 0)
            prob = s.prob[...]
            dprob = dot_nt(grad, s.value[...])
            weighted = prob * dprob
            inner = jnp.sum(weighted, -1, keepdims=True)
            draw = (weighted - prob * inner).astype(BF16)
            dq = (dot(draw, s.key[...]) * 0.125).reshape(8, SHORT, 128)
            for index in range(8):
                s.dq_out[index] = self.pack_one(dq[index])
            dkey = dot_tn(draw, s.query[...].reshape(count, 128))
            dvalue = dot_tn(prob, grad)
        both = jnp.where(own, dkey, pltpu.roll(dvalue, 64, 1)).astype(BF16)
        both = both.reshape(8, 2, self.rows, 128)
        for which in range(2):
            s.dkv_part[which] = both[:, which]

    def _merge(self):
        s = self.s
        return remote(
            s.dkv_part.at[1 - self.at.core], s.dkv_other, s.sems.at[14, 0], s.sems.at[14, 1], self.at.partner()
        )

    def merge_start(self):
        self.at.start(self._merge(), (self.index, 14))

    def merge(self):
        s = self.s
        self.at.finish(self._merge(), (self.index, 14))
        s.dkv_out[...] = (s.dkv_part[self.at.core].astype(F32) + s.dkv_other[...].astype(F32)).astype(BF16)

    def project_back(self):
        i, s, rows = self.index, self.s, self.rows
        cosine, sine = self.angles()
        low = lanes((rows, 128)) < 64
        back = jnp.zeros((rows, D), F32)
        for group in range(GROUPS):
            even, odd = s.dkv_in[2 * group].astype(F32), s.dkv_in[2 * group + 1].astype(F32)
            key = jnp.where(low, even, odd)
            key = key * cosine - half_turn(key) * sine
            value = pltpu.roll(jnp.where(low, odd, even), 64, 1)
            query = unpack_pair(s.dq_in[2 * group], s.dq_in[2 * group + 1], rows)
            query = query * cosine - half_turn(query) * sine
            for which, piece in enumerate((query, key, value)):
                place = 4 * which + group
                column = 128 * (place % 6)
                s.dproj[place // 6, :, column : column + 128] = piece.astype(BF16)
        for part in range(2):
            back = back + dot_nt(s.dproj[part], self.r.wqkv[i, :, 768 * part : 768 * part + 768])
        normal, scale = s.normal[0], s.scale[0][:, :1]
        self.r.gsum[2 * i : 2 * i + 1, :] = jnp.sum(back * normal, 0, keepdims=True)
        return s.dfirst[...] + normalize_back(back, normal, scale, self.gain(0))


    def _swap(self, which):
        s, other = self.s, 1 - self.at.core
        src, dst = (
            (s.glow, s.glow_in), (s.n2, s.n2_in), (s.act.at[other], s.act_in), (s.dhid.at[other], s.dhid_in),
            (s.mixed, s.mixed_in), (s.dv1.at[other], s.dv1_in), (s.n1, s.n1_in), (s.dproj.at[other], s.dproj_in),
        )[which]
        return remote(src, dst, s.sems.at[15, which], s.sems.at[16, which], self.at.partner())

    def swap(self, steps):
        for which in steps:
            self.at.start(self._swap(which), (self.index, 10, which))

    def swapped(self, steps):
        for which in steps:
            self.at.finish(self._swap(which), (self.index, 10, which))

    def grads_feed(self, total):
        s, core = self.s, self.at.core
        for part in range(4):
            at = slice(256 * part, 256 * part + 256)
            total.put_rows(
                part, dot_tn(s.act[core, :, at], s.glow[...]) + dot_tn(s.act_in[:, at], s.glow_in[...])
            )
        for part in range(2):
            at = slice(512 * part, 512 * part + 512)
            up = dot_tn(s.n2[...], s.dhid[core, :, at]) + dot_tn(s.n2_in[...], s.dhid_in[:, at])
            total.put_columns(4 + 2 * part, up[:, :256])
            total.put_columns(5 + 2 * part, up[:, 256:])
        total.put_columns(8, dot_tn(s.mixed[...], s.dv1[core]) + dot_tn(s.mixed_in[...], s.dv1_in[...]))

    def grads_attention(self, total):
        s, core = self.s, self.at.core
        grad = dot_tn(s.n1[...], s.dproj[core]) + dot_tn(s.n1_in[...], s.dproj_in[...])
        for part in range(3):
            total.put_columns(part, grad[:, 256 * part : 256 * part + 256])


class Total:
    def __init__(self, at, own, index, kind, result):
        self.at, self.s, self.index, self.kind, self.result = at, own, index, kind, result
        self.units = own.full.shape[-1] // 128

    def put_rows(self, unit, values):
        part, column = unit // self.units, unit % self.units * 128
        values = values.astype(BF16)
        for group in range(4):
            self.s.grads[part, group, :, :, :, column : column + 128] = values[
                :, 128 * group : 128 * group + 128
            ].reshape(4, 4, 16, 128)

    def put_columns(self, unit, values):
        part, column = unit // self.units, unit % self.units * 128
        values = values.astype(BF16)
        for group in range(2):
            self.s.grads[part, 2 * group : 2 * group + 2, :, :, :, column : column + 128] = values[
                :, 128 * group : 128 * group + 128
            ].reshape(2, 4, 4, 16, 128)

    def _scatter(self, part, stage, distance):
        s, axis = self.s, ORDERS[part][stage]
        to = lax.rem(self.at.at[axis] + distance, 4)
        src = (s.grads, s.sum1, s.sum2)[stage].at[part, to]
        dst = (s.part0, s.part1, s.part2)[stage].at[part, distance - 1]
        slot = 3 * part + distance - 1
        return remote(src, dst, s.sems.at[2 * stage, slot], s.sems.at[2 * stage + 1, slot], self.at.peer(axis, distance))

    def _gather(self, part, stage, distance):
        s, axis = self.s, ORDERS[part][stage]
        place = s.full.at[(part, *[self.at.at[a] for a in ORDERS[part]][: stage + 1])]
        slot = 3 * part + distance - 1
        send, recv = s.sems.at[6 + 2 * stage, slot], s.sems.at[7 + 2 * stage, slot]
        return remote(place, place, send, recv, self.at.peer(axis, distance))

    def _relay(self, part):
        src, dst = self.s.full.at[part], self.result.at[self.index, self.at.core, part]
        return remote(src, dst, self.s.sems.at[12, part], self.s.sems.at[12, 3 + part], self.at.partner())

    def _store(self, part):
        dst = self.result.at[self.index, self.at.core, part]
        return pltpu.make_async_copy(self.s.full.at[part], dst, self.s.sems.at[12, 6 + part])

    def _all(self, make, act, name, stage):
        for part in range(3):
            for distance in (1, 2, 3):
                act(make(part, stage, distance), (self.index, self.kind, name, part, stage, distance))

    def scatter(self, stage):
        self._all(self._scatter, self.at.start, 0, stage)

    def scattered(self, stage):
        s = self.s
        for part in range(3):
            for distance in (1, 2, 3):
                self.at.finish(self._scatter(part, stage, distance), (self.index, self.kind, 0, part, stage, distance))
            mine = [self.at.at[a] for a in ORDERS[part]]
            src = (s.grads, s.sum1, s.sum2)[stage]
            got = (s.part0, s.part1, s.part2)[stage]
            total = src[part, mine[stage]].astype(F32)
            for distance in range(3):
                total = total + got[part, distance].astype(F32)
            total = total.astype(BF16)
            if stage == 0:
                s.sum1[part] = total
            elif stage == 1:
                s.sum2[part] = total
            else:
                s.full[(part, *mine)] = total
            for distance in (1, 2, 3):
                if stage < 2:
                    copy = self._scatter(part, stage + 1, distance)
                    self.at.start(copy, (self.index, self.kind, 0, part, stage + 1, distance))
                else:
                    self.at.start(self._gather(part, 2, distance), (self.index, self.kind, 1, part, 2, distance))

    def gathered(self, stage):
        for part in range(3):
            for distance in (1, 2, 3):
                self.at.finish(self._gather(part, stage, distance), (self.index, self.kind, 1, part, stage, distance))
            if stage:
                for distance in (1, 2, 3):
                    copy = self._gather(part, stage - 1, distance)
                    self.at.start(copy, (self.index, self.kind, 1, part, stage - 1, distance))
            else:
                self.at.start(self._relay(part), (self.index, self.kind, 2, part))
                self._store(part).start()
                self.at.sending.append(self._store(part).wait)


def vmem(**shapes):
    return {name: pltpu.VMEM(shape, kind) for name, (shape, kind) in shapes.items()}


def layer_scratch(index, rows):
    length, half = SEQ * rows, padded(rows)
    message = rows + (NOTE if index == 0 else 0)
    shapes = vmem(
        kv_out=((8, message, 128), BF16), kv_in=((SEQ, message, 128), BF16),
        q_out=((8, half, 128), BF16), q_in=((8, half, 128), BF16),
        dm_out=((8, half, 128), BF16), dm_in=((8, half, 128), BF16),
        mix_out=((8, half, 128), BF16), mix_in=((8, half, 128), BF16),
        dq_out=((8, half, 128), BF16), dq_in=((8, half, 128), BF16),
        dkv_part=((2, 8, rows, 128), BF16), dkv_other=((8, rows, 128), BF16),
        dkv_out=((8, rows, 128), BF16), dkv_in=((8, rows, 128), BF16),
        query=((8, rows, 128), BF16), key=((length, 128), BF16), value=((length, 128), BF16),
        prob=((8, rows, length) if index == 0 else (8 * rows, length), BF16),
        normal=((2, rows, D), F32), scale=((2, rows, 128), F32),
        slope=((rows, FF), F32), dfirst=((rows, D), F32),
        n1=((rows, D), BF16), n2=((rows, D), BF16), mixed=((rows, D), BF16), glow=((rows, D), BF16),
        act=((2, rows, FF // 2), BF16), dhid=((2, rows, FF // 2), BF16),
        dv1=((2, rows, 256), BF16), dproj=((2, rows, 768), BF16),
        n1_in=((rows, D), BF16), n2_in=((rows, D), BF16), mixed_in=((rows, D), BF16), glow_in=((rows, D), BF16),
        act_in=((rows, FF // 2), BF16), dhid_in=((rows, FF // 2), BF16),
        dv1_in=((rows, 256), BF16), dproj_in=((rows, 768), BF16),
        column=((8, rows, 128), F32), line=((8, length), F32),
    )
    shapes.update(sems=pltpu.SemaphoreType.DMA((17, 8)))
    return shapes


def total_scratch(width):
    shapes = vmem(
        grads=((3, 4, 4, 4, 16, width), BF16),
        part0=((3, 3, 4, 4, 16, width), BF16), sum1=((3, 4, 4, 16, width), BF16),
        part1=((3, 3, 4, 16, width), BF16), sum2=((3, 4, 16, width), BF16),
        part2=((3, 3, 16, width), BF16),
        full=((3, 4, 4, 4, 16, width), BF16),
    )
    shapes.update(sems=pltpu.SemaphoreType.DMA((13, 9)))
    return shapes


def common_scratch():
    shapes = vmem(
        tokens=((LONG, D), BF16), cot=((LONG, D), BF16), seg=((1, LONG), jnp.int32), gains=((2, 2, D), BF16),
        offsets=((2, LONG, 128), F32), firsts=((2, 2 * SEQ, 128), F32),
        wqkv=((2, D, 3 * D), BF16), wout=((2, D, D), BF16),
        wup=((2, D, FF), BF16), wdown=((2, FF, D), BF16),
        dkey=((SEQ * LONG, 128), F32), dvalue=((SEQ * LONG, 128), F32),
        second=((4, LONG + 8, 128), F32), share=((4, SHORT + 8, 128), F32),
        work=((4, LONG, 128), F32), spread=((4, LONG, 128), F32),
        tail=((4, 8, 128), F32), ahead=((4, 8, 128), F32),
        output=((LONG, D), BF16), result=((LONG, D), F32),
        gsum=((8, D), F32), gain_in=((4, 4, 8, D), F32), gain_out=((3, 8, D), F32),
    )
    shapes.update(more=pltpu.SemaphoreType.DMA((6, 20)))
    return shapes


SPACES = (
    common_scratch(), layer_scratch(0, LONG), layer_scratch(1, SHORT),
    total_scratch(384), total_scratch(128), total_scratch(384), total_scratch(128),
)


def body(*refs):
    spaces, place = [], 15
    for part in SPACES:
        spaces.append(types.SimpleNamespace(**dict(zip(part, refs[place : place + len(part)]))))
        place += len(part)
    at = Place()
    steps(at, spaces, *refs[:15])
    for wait in at.coming.values():
        wait()
    for wait in at.sending:
        wait()


def steps(
    at, spaces, tokens, seg, wqkv, wout, wup, wdown, gains, cot, offsets, firsts,
    output, tokens_grad, feed_sums, attention_sums, gain_sum,
):
    ref = spaces[0]
    more = ref.more
    full, short = Layer(at, ref, spaces[1], 0, LONG), Layer(at, ref, spaces[2], 1, SHORT)
    full_feed, full_heads = Total(at, spaces[3], 0, 20, feed_sums), Total(at, spaces[4], 0, 21, attention_sums)
    short_feed, short_heads = Total(at, spaces[5], 1, 20, feed_sums), Total(at, spaces[6], 1, 21, attention_sums)

    pairs = [
        (tokens, ref.tokens), (gains, ref.gains), (wqkv.at[0], ref.wqkv.at[0]),
        (offsets, ref.offsets), (firsts, ref.firsts), (seg, ref.seg),
        (wout.at[0], ref.wout.at[0]), (wup.at[0], ref.wup.at[0]), (wdown.at[0], ref.wdown.at[0]),
        (wqkv.at[1], ref.wqkv.at[1]), (cot, ref.cot),
        (wout.at[1], ref.wout.at[1]), (wup.at[1], ref.wup.at[1]), (wdown.at[1], ref.wdown.at[1]),
    ]
    loads = [pltpu.make_async_copy(src, dst, more.at[0, step]) for step, (src, dst) in enumerate(pairs)]
    for load in loads:
        load.start()
    waiting = list(range(len(loads)))

    def loaded(count):
        while waiting and waiting[0] < count:
            loads[waiting.pop(0)].wait()

    at.sending.append(lambda: loaded(len(loads)))
    barrier = pltpu.get_barrier_semaphore()
    greeted = at.greet(barrier)

    loaded(6)
    inputs = ref.tokens[...].astype(F32)
    full.project(inputs)
    line = ref.seg[...].astype(F32)
    high = jnp.floor(line * (1.0 / 64.0))
    rows = jnp.concatenate([high, line - 64.0 * high, jnp.zeros((6, LONG), F32)], 0)
    third = jnp.where(sublanes((LONG, 128)) == 3 * lanes((LONG, 128)), 1.0, 0.0)
    picked = dot(rows, third)
    wide = jnp.concatenate([rows[:, 128:], jnp.zeros((8, 112), F32)], 1)
    note = jnp.concatenate([rows[0:2, :128], wide[0:2], picked[0:2], jnp.zeros((10, 128), F32)], 0).astype(BF16)
    for head in range(8):
        full.s.kv_out[head, LONG:] = note
    pl.semaphore_wait(barrier, greeted)
    full.send(KV)
    full.send(Q)

    def segments():
        notes = [full.s.kv_in[block, LONG:, :].astype(F32) for block in range(SEQ)]
        for block, code in enumerate(notes):
            long = jnp.concatenate([64.0 * code[0:1] + code[1:2], 64.0 * code[2:3, :16] + code[3:4, :16]], 1)
            full.s.line[0:1, LONG * block : LONG * block + LONG] = long
            short.s.line[0:1, SHORT * block : SHORT * block + SHORT] = (64.0 * code[4:5] + code[5:6])[:, :SHORT]
        for layer in (full, short):
            rows = layer.rows
            equal = lanes((rows, rows)) == sublanes((rows, rows))
            for pair in range(8):
                code = full.s.kv_in[2 * pair + at.core, LONG:, :].astype(F32)
                if layer is full:
                    line = jnp.concatenate([64.0 * code[0:1] + code[1:2], 64.0 * code[2:3, :16] + code[3:4, :16]], 1)
                else:
                    line = (64.0 * code[4:5] + code[5:6])[:, :SHORT]
                column = jnp.sum(jnp.where(equal, line, 0.0), 1, keepdims=True)
                layer.s.column[pair] = jnp.broadcast_to(column, (rows, 128))

    def attention(layer):
        layer.receive_keys()
        layer.receive(Q)
        if layer is full:
            segments()
        layer.split_heads()
        layer.attend()
        layer.send(MIX)
        layer.receive(MIX)

    attention(full)
    loaded(9)
    second = ref.second
    spill(second, 8, full.feed_forward(inputs))

    def halo():
        return remote(second.at[:, pl.ds(LONG, 8), :], ref.tail, more.at[1, 0], more.at[1, 1], at.along(1))

    at.start(halo(), (3, 0))
    loaded(11)
    work = ref.work
    spill(work, 0, ref.cot[...].astype(F32))
    grad_short = jnp.concatenate(
        [every_third(work, 0, g) + every_third(work, 1, g) + every_third(work, 2, g) for g in range(GROUPS)], 1
    )
    at.finish(halo(), (3, 0))
    second[:, 0:8, :] = jnp.where(at.seq == 0, 0.0, ref.tail[...])
    pooled = jnp.concatenate(
        [
            (every_third(second, 6, g) + every_third(second, 7, g) + every_third(second, 8, g)) / 3.0
            for g in range(GROUPS)
        ],
        1,
    )
    short.project(pooled)
    short.send(KV)
    short.send(Q)
    loaded(14)
    attention(short)
    result = short.feed_forward(pooled)

    def backward(layer, total, grad, between):
        layer.feed_back(grad)
        layer.send(DM)
        layer.swap((0, 1, 2, 3, 4, 5, 6))
        between(0)
        layer.swapped((0, 1, 2, 3, 4, 5, 6))
        layer.grads_feed(total)
        total.scatter(0)
        between(1)
        layer.receive(DM)
        layer.attend_back()
        layer.merge_start()
        layer.send(DQ)
        layer.merge()
        layer.send(DKV)
        between(2)
        layer.receive(DQ)
        layer.receive(DKV)
        back = layer.project_back()
        layer.swap((7,))
        return back

    spread = ref.spread

    def finish_output():
        for group in range(GROUPS):
            at_lanes = slice(128 * group, 128 * group + 128)
            for step in range(3):
                spread[group, pl.ds(step, SHORT, 3), :] = every_third(second, 8 + step, group) + result[:, at_lanes]
            ref.output[:, at_lanes] = spread[group].astype(BF16)
        store = pltpu.make_async_copy(ref.output, output, more.at[0, 14])
        store.start()
        at.sending.append(store.wait)

    def between_short(point):
        if point == 0:
            finish_output()

    share = ref.share
    spill(share, 0, backward(short, short_feed, grad_short, between_short) * (1.0 / 3.0))

    def halo_back():
        return remote(share.at[:, pl.ds(0, 8), :], ref.ahead, more.at[1, 2], more.at[1, 3], at.along(SEQ - 1))

    at.start(halo_back(), (3, 1))
    short.swapped((7,))
    short.grads_attention(short_heads)
    short_heads.scatter(0)
    short_feed.scattered(0)
    at.finish(halo_back(), (3, 1))
    share[:, SHORT:, :] = jnp.where(at.seq == SEQ - 1, 0.0, ref.ahead[...])
    for group in range(GROUPS):
        own, following = share[group, 0:SHORT, :], share[group, 1 : SHORT + 1, :]
        for step, piece in enumerate((own, following, following)):
            spread[group, pl.ds(step, SHORT, 3), :] = every_third(work, step, group) + piece
    grad_full = jnp.concatenate([spread[group] for group in range(GROUPS)], 1)

    def between_full(point):
        if point == 0:
            short_feed.scattered(1)
        elif point == 1:
            short_heads.scattered(0)
            short_feed.scattered(2)
        else:
            short_feed.gathered(2)
            short_heads.scattered(1)
            short_feed.gathered(1)
            full_feed.scattered(0)
            short_heads.scattered(2)

    ref.result[...] = backward(full, full_feed, grad_full, between_full)
    store = pltpu.make_async_copy(ref.result, tokens_grad, more.at[0, 15])
    store.start()
    at.sending.append(store.wait)
    full_feed.scattered(1)
    full.swapped((7,))
    full.grads_attention(full_heads)
    full_heads.scatter(0)

    gsum, gain_in, gain_out = ref.gsum, ref.gain_in, ref.gain_out

    def gain_copy(axis, distance):
        src = gsum if axis == 0 else gain_out.at[axis - 1]
        return remote(
            src, gain_in.at[axis, at.at[axis]], more.at[2, 3 * axis + distance], more.at[3, 3 * axis + distance],
            at.peer(axis, distance),
        )

    def gain_step(axis):
        for distance in (1, 2, 3):
            at.start(gain_copy(axis, distance), (4, axis, distance))
        gain_in[axis, at.at[axis]] = gsum[...] if axis == 0 else gain_out[axis - 1]

    def gain_done(axis):
        for distance in (1, 2, 3):
            at.finish(gain_copy(axis, distance), (4, axis, distance))
        return (gain_in[axis, 0] + gain_in[axis, 1]) + (gain_in[axis, 2] + gain_in[axis, 3])

    gsum[4:, :] = jnp.zeros((4, D), F32)
    gain_step(0)
    full_feed.scattered(2)
    short_heads.gathered(2)
    full_heads.scattered(0)
    short_feed.gathered(0)
    gain_out[0] = gain_done(0)
    gain_step(1)
    full_feed.gathered(2)
    short_heads.gathered(1)
    full_heads.scattered(1)
    gain_out[1] = gain_done(1)
    gain_step(2)
    full_feed.gathered(1)
    full_heads.scattered(2)
    short_heads.gathered(0)
    gain_in[3, 0] = gain_done(2)
    gain_swap = remote(gain_in.at[3, 0], gain_in.at[3, 1], more.at[1, 4], more.at[1, 5], at.partner())
    at.start(gain_swap, (4, 3, 0))
    full_heads.gathered(2)
    full_heads.gathered(1)
    full_feed.gathered(0)
    full_heads.gathered(0)
    at.finish(gain_swap, (4, 3, 0))
    gain_out[2] = gain_in[3, 0] + gain_in[3, 1]
    store = pltpu.make_async_copy(gain_out.at[2], gain_sum, more.at[0, 16])
    store.start()
    at.sending.append(store.wait)


def tables():
    freq = 10000.0 ** (-np.arange(32) / 32.0)
    freq = np.tile(freq, 4)[None, :]
    offset = np.arange(LONG)[:, None] * freq
    first = np.concatenate([np.arange(SEQ) * LONG, np.arange(SEQ) * SHORT])[:, None] * freq
    return (
        np.stack([np.cos(offset), np.sin(offset)]).astype(np.float32),
        np.stack([np.cos(first), np.sin(first)]).astype(np.float32),
    )


def widen_body(
    feed, heads, gain, output, grad, qkv, out, up, down, gains, output_too, grad_too,
    feed_in, heads_in, gain_in, gain_out, down_out, up_out, out_out, qkv_out, sems,
):
    def place(step):
        return step // 2, step % 2

    loads, stores = [], []
    small = [
        pltpu.make_async_copy(gain, gain_in, sems.at[0, 0]),
        pltpu.make_async_copy(output, output_too.at[0], sems.at[0, 1]),
        pltpu.make_async_copy(grad, grad_too.at[0], sems.at[0, 2]),
    ]
    for step in range(4):
        block, half = place(step)
        for part in range(3):
            loads.append(pltpu.make_async_copy(feed.at[block, half, part], feed_in.at[step, part], sems.at[1 + step, part]))
        loads.append(pltpu.make_async_copy(heads.at[block, half], heads_in.at[step], sems.at[1 + step, 3]))
    for copy in loads + small:
        copy.start()
    small[0].wait()
    gain_out[...] = gain_in[0:4, :].reshape(2, 2, D)
    small[0] = pltpu.make_async_copy(gain_out, gains, sems.at[0, 3])
    small[0].start()
    for step in range(4):
        block, half = place(step)

        def put(copy_to, source, slot):
            copy = pltpu.make_async_copy(source, copy_to, sems.at[5 + step, slot])
            copy.start()
            stores.append(copy)

        for unit in range(9):
            if unit % 3 == 0:
                loads[4 * step + unit // 3].wait()
            lane = slice(128 * (unit % 3), 128 * (unit % 3) + 128)
            tiles = feed_in.at[step, unit // 3]
            if unit < 4:
                rows = slice(256 * unit, 256 * unit + 256)
                for group in range(4):
                    values = tiles[group, :, :, :, lane].reshape(256, 128).astype(F32)
                    down_out[step, rows, 128 * group : 128 * group + 128] = values
            else:
                for group in range(2):
                    values = tiles[2 * group : 2 * group + 2, :, :, :, lane].reshape(512, 128).astype(F32)
                    if unit < 8:
                        column = 256 * (unit - 4) + 128 * group
                        up_out[step, :, column : column + 128] = values
                    else:
                        out_out[step, :, 128 * group : 128 * group + 128] = values
            if unit == 3:
                put(down.at[block, pl.ds(1024 * half, 1024), :], down_out.at[step], 0)
            elif unit == 7:
                put(up.at[block, :, pl.ds(1024 * half, 1024)], up_out.at[step], 1)
            elif unit == 8:
                put(out.at[block, :, pl.ds(256 * half, 256)], out_out.at[step], 2)
        loads[4 * step + 3].wait()
        for unit in range(3):
            for group in range(2):
                column = 256 * unit + 128 * group
                tiles = heads_in[step, unit, 2 * group : 2 * group + 2]
                qkv_out[step, :, column : column + 128] = tiles.reshape(512, 128).astype(F32)
        put(qkv.at[block, :, pl.ds(768 * half, 768)], qkv_out.at[step], 3)
    for copy in stores + small:
        copy.wait()


def widen(feed, heads, gain, output, grad):
    anywhere = pl.BlockSpec(memory_space=pl.ANY)
    return pl.pallas_call(
        widen_body,
        out_shape=(
            jax.ShapeDtypeStruct((2, D, 3 * D), F32),
            jax.ShapeDtypeStruct((2, D, D), F32),
            jax.ShapeDtypeStruct((2, D, FF), F32),
            jax.ShapeDtypeStruct((2, FF, D), F32),
            jax.ShapeDtypeStruct((2, 2, D), F32),
            jax.ShapeDtypeStruct((1, LONG, D), BF16),
            jax.ShapeDtypeStruct((1, LONG, D), F32),
        ),
        in_specs=[anywhere] * 5,
        out_specs=(anywhere,) * 7,
        scratch_shapes=[
            pltpu.VMEM((4, 3, 4, 4, 4, 16, 384), BF16),
            pltpu.VMEM((4, 3, 4, 4, 4, 16, 128), BF16),
            pltpu.VMEM((8, D), F32),
            pltpu.VMEM((2, 2, D), F32),
            pltpu.VMEM((4, 1024, 512), F32),
            pltpu.VMEM((4, 512, 1024), F32),
            pltpu.VMEM((4, 512, 256), F32),
            pltpu.VMEM((4, 512, 768), F32),
            pltpu.SemaphoreType.DMA((9, 4)),
        ],
        compiler_params=pltpu.CompilerParams(vmem_limit_bytes=56 * 2**20),
        name="widen",
    )(feed, heads, gain, output, grad)


def per_device(tokens, segment, w_qkv, w_out, w_up, w_down, gains, cotangent):
    offsets, firsts = tables()
    anywhere = pl.BlockSpec(memory_space=pl.ANY)
    output, tokens_grad, feed, heads, gain = pl.pallas_call(
        body,
        out_shape=(
            jax.ShapeDtypeStruct((LONG, D), BF16),
            jax.ShapeDtypeStruct((LONG, D), F32),
            jax.ShapeDtypeStruct((2, 2, 3, 4, 4, 4, 16, 384), BF16),
            jax.ShapeDtypeStruct((2, 2, 3, 4, 4, 4, 16, 128), BF16),
            jax.ShapeDtypeStruct((8, D), F32),
        ),
        in_specs=[anywhere] * 10,
        out_specs=(anywhere,) * 5,
        scratch_shapes=[shape for part in SPACES for shape in part.values()],
        compiler_params=pltpu.CompilerParams(
            collective_id=0, has_side_effects=True, vmem_limit_bytes=62 * 2**20
        ),
        name="layers",
    )(
        tokens[0], segment, w_qkv, w_out, w_up, w_down, gains, cotangent[0],
        jnp.asarray(offsets), jnp.asarray(firsts),
    )
    qkv, out, up, down, gain, output, tokens_grad = widen(feed, heads, gain, output, tokens_grad)
    return output, tokens_grad, qkv, out, up, down, gain


def solution(mesh):
    return jax.shard_map(
        per_device,
        mesh=mesh,
        in_specs=(
            P("row", "seq", None),
            P("row", "seq"),
            P(),
            P(),
            P(),
            P(),
            P(),
            P("row", "seq", None),
        ),
        out_specs=(P("row", "seq", None), P("row", "seq", None), P(), P(), P(), P(), P()),
        check_vma=False,
    )
```

time: 842 us -> 172 us (0.20); the launches traced: 832 us -> 172 us
  waiting for transfers between devices: 413 us -> 0 us
  blocking collectives: 172 us -> 0 us
  Pallas kernels: 0 us -> 171 us
  matrix products: 131 us -> 0 us
  local copies, waits for them, and re-layouts: 63.1 us -> 0 us
  other arithmetic: 31.9 us -> 0 us
  between operations: 17.5 us -> 0.82 us
    pallas_call x0 -> x2, Pallas kernels: none -> 171 us  [the longest x1 156 us: per_device(): pl.pallas_call(body, out_shape=(jax.ShapeDtypeStruct((LONG, D), BF16), ja...]
    psum x1 -> x0, waiting for transfers between devices: 165 us -> none  [per_device(): lax.psum((full_grads[0], full_grads[1], full_grads[2], full_grads[3], ful...]
    reduce_scatter x2 -> x0, waiting for transfers between devices: 146 us -> none  [the longest x1 73.8 us: block_backward(): lax.psum_scatter(grad_keys.astype(jnp.bfloat16), 'seq', scatter_dimension...]
    dot_general x34 -> x0, matrix products: 122 us -> none  [the longest x2 25 us: attention_grads(): jnp.einsum('rhqk,rqhe->rkhe', grad_raw, query.reshape(row_count, stretch_...]
    unnamed x9 -> x0, waiting for transfers between devices: 79.4 us -> none
    psum x1 -> x0, blocking collectives: 67 us -> none  [per_device(): lax.psum((full_grads[0], full_grads[1], full_grads[2], full_grads[3], ful...]
    unnamed x1 -> x0, blocking collectives: 62.9 us -> none
    all_gather x2 -> x0, blocking collectives: 41.6 us -> none  [the longest x1 23.1 us: block_forward(): lax.all_gather(key_part, 'seq', axis=1, tiled=True)]
  transfers between devices with their start and end apart: 9 -> 0, of which waited for: 7 -> 0; matrix products, arithmetic and copies ran while one was open for 13% -> 0% of each run, Pallas kernels for 0% -> 0%
where the time goes in v1:
time: 172 us
  Pallas kernels  171 us (99%)
    pallas_call x1, Pallas kernels, per_device(): pl.pallas_call(body, out_shape=(jax.ShapeDtypeStruct((LONG, D), BF16), ja...  156 us
    pallas_call x1, Pallas kernels, widen(): pl.pallas_call(widen_body, out_shape=(jax.ShapeDtypeStruct((2, D, 3 * D),...  14.8 us

profile of v1, /device:TPU:1, one launch (start us, length us, event | category | flops | bytes accessed | tf_op | source)
XLA Modules:
  0.0 171.6 jit_solution(10456871419646968155)
XLA Ops:
  0.6 155.9 %layers.1 = (bf16[144,512]{1,0:T(8,128)(2,1)}, f32[144,512]{1,0:T(8,128)}, bf16[2,2,3,4,4,4,16,384]{7,6,5,4,3,2,1,0:T(8,128)(2,1)}, bf16[2,2,3,4,4,4,16,128]{7,6,5,4,3,2,1,0:T(8,128)(2,1)}, f32[8,512]{1,0:T(8,128)}) custom-call(bf16[144,512]{1,0:T(8,128)(2,1)} %bitcast.2, s32[1,144]{1,0:T(1,128)} %refs_1_.1, bf16[2,512,1536]{2,1,0:T(8,128)(2,1)} %refs_2_.1, ...), custom_call_target="tpu_custom_call" | custom-call | tf_op jit(solution)/shard_map/layers/pallas_call | solution.py:1026
  156.6 14.8 %widen.1 = (f32[2,512,1536]{2,1,0:T(8,128)}, f32[2,512,512]{2,1,0:T(8,128)}, f32[2,512,2048]{2,1,0:T(8,128)}, f32[2,2048,512]{2,1,0:T(8,128)}, f32[2,2,512]{2,1,...) custom-call(bf16[2,2,3,4,4,4,16,384]{7,6,5,4,3,2,1,0:T(8,128)(2,1)} %get-tuple-element.19.feed, ...), custom_call_target="tpu_custom_call" | custom-call | tf_op jit(solution)/shard_map/widen/pallas_call | solution.py:994

commit v2 on v1

v2 whole, which is shorter than its diff:
```python
import types

import jax
import jax.numpy as jnp
import numpy as np
from jax import lax
from jax.experimental import pallas as pl
from jax.experimental.pallas import tpu as pltpu
from jax.sharding import PartitionSpec as P

MESH = pl.DeviceIdType.MESH
F32 = jnp.float32
BF16 = jnp.bfloat16

SEQ = 16
LONG = 144
SHORT = 48
D = 512
FF = 2048
GROUPS = 4
NOTE = 16
KV, Q, DM, MIX, DKV, DQ = range(6)
SEVEN = tuple(range(7))
UNITS = (3, 4, 1)
HOP, BACK = 9, 10
X, Y, Z = range(3)
ORDERS = ((X, Y, Z), (Y, Z, X), (Z, X, Y))


def dot(left, right):
    return jnp.dot(left, right, preferred_element_type=F32)


def dot_nt(left, right):
    return lax.dot_general(left, right, (((1,), (1,)), ((), ())), preferred_element_type=F32)


def dot_tn(left, right):
    return lax.dot_general(left, right, (((0,), (0,)), ((), ())), preferred_element_type=F32)


def lanes(shape):
    return lax.broadcasted_iota(jnp.int32, shape, len(shape) - 1)


def sublanes(shape):
    return lax.broadcasted_iota(jnp.int32, shape, len(shape) - 2)


def normalize(values):
    center = values - jnp.mean(values, -1, keepdims=True)
    scale = lax.rsqrt(jnp.mean(center * center, -1, keepdims=True) + 1e-05)
    return center * scale, scale


def normalize_back(grad, normal, scale, gain):
    inner = grad * gain
    return scale * (
        inner
        - jnp.mean(inner, -1, keepdims=True)
        - normal * jnp.mean(inner * normal, -1, keepdims=True)
    )


def half_turn(tensor):
    up = pltpu.roll(tensor, 96, 1)
    down = pltpu.roll(tensor, 32, 1)
    return jnp.where(lanes(tensor.shape) % 64 < 32, -up, down)


def padded(rows):
    return -(-rows // 32) * 16


def seal(packed):
    rows = packed.shape[0]
    return jnp.concatenate([packed, jnp.zeros((padded(2 * rows) - rows, 128), F32)], 0).astype(BF16)


def pack_pair(pair):
    rows = pair.shape[0] // 2
    top, bottom = pair[:rows], pltpu.roll(pair[rows:], 64, 1)
    low = lanes(top.shape) < 64
    return seal(jnp.where(low, top, bottom)), seal(jnp.where(low, bottom, top))


def unpack_pair(even, odd, rows):
    even, odd = even.astype(F32)[: rows // 2], odd.astype(F32)[: rows // 2]
    low = lanes(even.shape) < 64
    return jnp.concatenate([jnp.where(low, even, odd), pltpu.roll(jnp.where(low, odd, even), 64, 1)], 0)


def unpack_one(packed, rows):
    packed = packed.astype(F32)[: rows // 2]
    return jnp.concatenate([packed, pltpu.roll(packed, 64, 1)], 0)


def spill(ref, first, values):
    for group in range(GROUPS):
        ref[group, first : first + values.shape[0], :] = values[:, 128 * group : 128 * group + 128]


def every_third(ref, first, group):
    return ref[group, pl.ds(first, SHORT, 3), :]


def remote(src, dst, send, recv, device):
    return pltpu.make_async_remote_copy(
        src_ref=src, dst_ref=dst, send_sem=send, recv_sem=recv, device_id=device, device_id_type=MESH
    )


class Place:
    def __init__(self):
        self.row = lax.axis_index("row")
        self.seq = lax.axis_index("seq")
        self.core = lax.rem(self.row, 2)
        self.at = (self.row // 2, lax.rem(self.seq, 4), self.seq // 4)
        self.head = lax.rem(self.seq, 8)
        self.same = (self.seq // 8 == self.core) & (lax.rem(self.seq, 2) == self.core)
        self.sending, self.coming = [], {}

    def peer(self, axis, distance):
        to = lax.rem(self.at[axis] + distance, 4)
        if axis == X:
            return (to * 2 + self.core, self.seq)
        if axis == Y:
            return (self.row, self.at[Z] * 4 + to)
        return (self.row, to * 4 + self.at[Y])

    def partner(self):
        return (self.row + 1 - 2 * self.core, self.seq)

    def along(self, distance):
        return (self.row, lax.rem(self.seq + distance, SEQ))

    def holder(self, head):
        device = (2 * self.at[X] + lax.rem(self.seq, 2), 8 * self.core + head)
        return device, self.same & (self.head == head)

    def owner(self, index):
        device = (2 * self.at[X] + self.seq // 8, 2 * index + self.core)
        return device, self.same & (self.seq // 2 == index)

    def start(self, copy, key):
        copy.start()
        self.sending.append(copy.wait_send)
        self.coming[key] = copy.wait_recv

    def finish(self, copy, key):
        self.coming.pop(key)
        copy.wait_recv()

    def greet(self, barrier):
        for make in (self.holder, self.owner):
            for index in range(8):
                device, same = make(index)

                @pl.when(jnp.logical_not(same))
                def _():
                    pl.semaphore_signal(barrier, inc=1, device_id=device, device_id_type=MESH)

        others = [self.partner(), self.along(1), self.along(SEQ - 1)]
        others += [self.peer(axis, distance) for axis in (X, Y, Z) for distance in (1, 2, 3)]
        for device in others:
            pl.semaphore_signal(barrier, inc=1, device_id=device, device_id_type=MESH)
        return 16 + len(others) - 2 * self.same.astype(jnp.int32)


COUNTS = [-(-2 * LONG * (pair + 1) // 128) * 128 for pair in range(8)]
FIRSTS = [sum(COUNTS[:pair]) for pair in range(8)]


class Layer:
    def __init__(self, at, ref, own, index, rows):
        self.at = at
        self.r = ref
        self.s = own
        self.index = index
        self.rows = rows
        self.slope = own.slope if index else ref.dkey


    def _buffers(self, kind):
        s = self.s
        return (
            (s.kv_out, s.kv_in), (s.q_out, s.q_in), (s.dm_out, s.dm_in),
            (s.mix_out, s.mix_in), (s.dkv_out, s.dkv_in), (s.dq_out, s.dq_in),
        )[kind]

    def _copy(self, kind, index):
        at, sems = self.at, self.s.sems
        out, into = self._buffers(kind)
        if kind in (KV, Q, DM):
            (device, same), slot = at.holder(index), at.seq // 2
            target = at.seq if kind == KV else slot
        else:
            (device, same), slot = at.owner(index), at.head
            target = slot
        recv = sems.at[2, slot] if kind == KV else sems.at[1, kind]
        return out.at[index], into.at[target], sems.at[0, kind], recv, device, same

    def send_one(self, kind, index):
        src, dst, send, recv, device, same = self._copy(kind, index)

        @pl.when(same)
        def _():
            pltpu.make_async_copy(src, dst, recv).start()

        @pl.when(jnp.logical_not(same))
        def _():
            remote(src, dst, send, recv, device).start()

    def send_rest(self, kind):
        self.at.sending.append(lambda: self.sent(kind))
        self.at.coming[(self.index, kind)] = lambda: self.receive(kind)

    def send(self, kind):
        begin = self.at.seq // 2 if kind in (KV, Q, DM) else self.at.head

        def one(step, carry):
            self.send_one(kind, lax.rem(step + begin, 8))
            return carry

        lax.fori_loop(0, 8, one, 0)
        self.send_rest(kind)

    def _wait(self, place, send, recv):
        return remote(place, place, send, recv, self.at.partner())

    def receive(self, kind):
        self.at.coming.pop((self.index, kind), None)
        sems = self.s.sems
        self._wait(self._buffers(kind)[1], sems.at[0, kind], sems.at[1, kind]).wait_recv()

    def sent(self, kind):
        out, sems = self._buffers(kind)[0], self.s.sems

        @pl.when(self.at.same)
        def _():
            self._wait(out.at[pl.ds(0, 7)], sems.at[0, kind], sems.at[1, kind]).wait_send()

        @pl.when(jnp.logical_not(self.at.same))
        def _():
            self._wait(out, sems.at[0, kind], sems.at[1, kind]).wait_send()

    def _relay(self, index):
        place = self.s.kv_in.at[2 * index + self.at.core]
        sems = self.s.sems
        return remote(place, place, sems.at[0, 6], sems.at[1, 6], self.at.partner())

    def receive_keys(self):
        self.at.coming.pop((self.index, KV), None)
        s = self.s

        def one(index, carry):
            self._wait(s.kv_in.at[0], s.sems.at[0, KV], s.sems.at[2, index]).wait_recv()
            self._relay(index).start()
            return carry

        lax.fori_loop(0, 8, one, 0)
        relayed = self._wait(s.kv_in.at[pl.ds(0, 8)], s.sems.at[0, 6], s.sems.at[1, 6])
        relayed.wait_recv()
        self.at.sending.append(relayed.wait_send)


    def angles(self):
        table, first = self.r.offsets, self.r.firsts
        place = self.index * SEQ + self.at.seq
        cos_a, sin_a = first[0, pl.ds(place, 1), :], first[1, pl.ds(place, 1), :]
        cos_b, sin_b = table[0, : self.rows, :], table[1, : self.rows, :]
        return cos_a * cos_b - sin_a * sin_b, sin_a * cos_b + cos_a * sin_b

    def gain(self, which):
        return self.r.gains[self.index, which : which + 1, :].astype(F32)

    def project(self, values, ready=None):
        s, rows = self.s, self.rows
        normal, scale = normalize(values)
        s.normal[0] = normal
        s.scale[0] = jnp.broadcast_to(scale, (rows, 128))
        normed = (normal * self.gain(0)).astype(BF16)
        s.n1[...] = normed
        cosine, sine = self.angles()
        low = lanes((rows, 128)) < 64
        weight = self.r.wqkv.at[self.index]
        for group in range(GROUPS):
            key = dot(normed, weight[:, 512 + 128 * group : 640 + 128 * group])
            value = dot(normed, weight[:, 1024 + 128 * group : 1152 + 128 * group])
            key = key * cosine + half_turn(key) * sine
            value = pltpu.roll(value, 64, 1)
            s.kv_out[2 * group, :rows] = jnp.where(low, key, value).astype(BF16)
            s.kv_out[2 * group + 1, :rows] = jnp.where(low, value, key).astype(BF16)
            query = dot(normed, weight[:, 128 * group : 128 * group + 128])
            query = (query * cosine + half_turn(query) * sine) * 0.125
            s.q_out[2 * group], s.q_out[2 * group + 1] = pack_pair(query)
        if ready is not None:
            ready()
        self.send(KV)
        self.send(Q)

    def native(self, shape):
        return (lanes(shape) // 64) == lax.rem(self.at.seq, 2)

    def pack_one(self, values):
        rows = self.rows // 2
        return seal(jnp.where(self.native((rows, 128)), values[:rows], pltpu.roll(values[rows:], 64, 1)))

    def split_heads(self):
        s, length = self.s, SEQ * self.rows
        both = s.kv_in[:, : self.rows, :].reshape(length, 128).astype(F32)
        own = self.native((length, 128))
        s.key[...] = jnp.where(own, both, 0.0).astype(BF16)
        s.value[...] = jnp.where(own, pltpu.roll(both, 64, 1), 0.0).astype(BF16)

    def attend(self):
        s, core = self.s, self.at.core
        for index in range(8):
            s.query[index] = unpack_one(s.q_in[index], self.rows).astype(BF16)
        if self.index == 0:
            for pair in reversed(range(8)):
                count = COUNTS[pair]
                score = dot_nt(s.query[pair], s.key[:count])
                first = (288 * pair) // 128 * 128
                column = s.column[pair][:, :1]
                allowed = s.line[0:1, :count] == column
                position = sublanes((LONG, count - first)) + (2 * pair + core) * LONG
                causal = lanes((LONG, count - first)) + first <= position
                if first:
                    head = jnp.where(allowed[:, :first], score[:, :first], -1e9)
                    tail = jnp.where(allowed[:, first:] & causal, score[:, first:], -1e9)
                    score = jnp.concatenate([head, tail], 1)
                else:
                    score = jnp.where(allowed & causal, score, -1e9)
                top = jnp.max(score, -1, keepdims=True)
                expo = jnp.exp(score - top)
                share = 1.0 / jnp.sum(expo, -1, keepdims=True)
                expo = expo.astype(BF16)
                s.expo[:, FIRSTS[pair] : FIRSTS[pair] + count] = expo
                s.part[pair] = jnp.broadcast_to(share, (LONG, 128))
                s.mix_out[pair] = self.pack_one(dot(expo, s.value[:count]) * share)
                self.send_one(MIX, pair)
            self.send_rest(MIX)
        else:
            count, length = 8 * SHORT, SEQ * SHORT
            score = dot_nt(s.query[...].reshape(count, 128), s.key[...])
            column = s.column[...].reshape(count, 128)[:, :1]
            row = lax.broadcasted_iota(jnp.int32, (8, SHORT, length), 1)
            block = lax.broadcasted_iota(jnp.int32, (8, SHORT, length), 0)
            position = (row + (2 * block + core) * SHORT).reshape(count, length)
            causal = lanes((count, length)) <= position
            score = jnp.where((s.line[0:1, :] == column) & causal, score, -1e9)
            top = jnp.max(score, -1, keepdims=True)
            expo = jnp.exp(score - top)
            share = 1.0 / jnp.sum(expo, -1, keepdims=True)
            expo = expo.astype(BF16)
            s.expo[...] = expo
            s.part[...] = jnp.broadcast_to(share, (count, 128)).reshape(8, SHORT, 128)
            mixed = (dot(expo, s.value[...]) * share).reshape(8, SHORT, 128)
            for index in range(8):
                s.mix_out[index] = self.pack_one(mixed[index])
            self.send(MIX)

    def feed_forward(self, values):
        i, s = self.index, self.s
        parts = [unpack_pair(s.mix_in[2 * g], s.mix_in[2 * g + 1], self.rows) for g in range(GROUPS)]
        mixed = jnp.concatenate(parts, 1).astype(BF16)
        s.mixed[...] = mixed
        first = values + dot(mixed, self.r.wout[i])
        normal, scale = normalize(first)
        s.normal[1] = normal
        s.scale[1] = jnp.broadcast_to(scale, (self.rows, 128))
        normed = (normal * self.gain(1)).astype(BF16)
        s.n2[...] = normed
        result = first
        for part in range(4):
            at = slice(512 * part, 512 * part + 512)
            hidden = dot(normed, self.r.wup[i, :, at])
            inner = 0.7978845608028654 * (hidden + 0.044715 * hidden * hidden * hidden)
            bend = jnp.tanh(inner)
            active = (0.5 * hidden * (1.0 + bend)).astype(BF16)
            slope = 0.5 * (1.0 + bend) + 0.5 * hidden * (1.0 - bend * bend) * (
                0.7978845608028654 * (1.0 + 3.0 * 0.044715 * hidden * hidden)
            )
            for column in range(4):
                place = self.rows * (4 * part + column)
                self.slope[place : place + self.rows, :] = slope[:, 128 * column : 128 * column + 128]
            s.act[part // 2, :, 512 * (part % 2) : 512 * (part % 2) + 512] = active
            result = result + dot(active, self.r.wdown[i, at, :])
        return result


    def feed_back(self, grad):
        i, s = self.index, self.s
        low = grad.astype(BF16)
        s.glow[...] = low
        back = jnp.zeros((self.rows, D), F32)
        for part in range(4):
            at = slice(512 * part, 512 * part + 512)
            active = dot_nt(low, self.r.wdown[i, at, :])
            places = [self.rows * (4 * part + column) for column in range(4)]
            slope = jnp.concatenate([self.slope[place : place + self.rows, :] for place in places], 1)
            hidden = (slope * active).astype(BF16)
            s.dhid[part // 2, :, 512 * (part % 2) : 512 * (part % 2) + 512] = hidden
            back = back + dot_nt(hidden, self.r.wup[i, :, at])
        normal, scale = s.normal[1], s.scale[1][:, :1]
        self.r.gsum[2 * i + 1 : 2 * i + 2, :] = jnp.sum(back * normal, 0, keepdims=True)
        first = grad + normalize_back(back, normal, scale, self.gain(1))
        s.dfirst[...] = first
        first_low = first.astype(BF16)
        s.dv1[0] = first_low[:, :256]
        s.dv1[1] = first_low[:, 256:]
        for group in range(GROUPS):
            weight = self.r.wout[i, 128 * group : 128 * group + 128, :]
            s.dm_out[2 * group], s.dm_out[2 * group + 1] = pack_pair(dot_nt(first_low, weight))
        self.send(DM)

    def attend_back(self, between):
        s, length = self.s, SEQ * self.rows
        own = self.native((length, 128))
        if self.index == 0:
            self.r.dkey[...] = jnp.zeros((length, 128), F32)
            self.r.dvalue[...] = jnp.zeros((length, 128), F32)
            for pair in reversed(range(8)):
                count = COUNTS[pair]
                share = s.part[pair]
                grad = (unpack_one(s.dm_in[pair], self.rows) * share).astype(BF16)
                expo = s.expo[:, FIRSTS[pair] : FIRSTS[pair] + count]
                weighted = expo * dot_nt(grad, s.value[:count])
                inner = jnp.sum(weighted, -1, keepdims=True) * share[:, :1]
                draw = (weighted - expo * inner).astype(BF16)
                s.dq_out[pair] = self.pack_one(dot(draw, s.key[:count]) * 0.125)
                self.r.dkey[:count] += dot_tn(draw, s.query[pair])
                self.r.dvalue[:count] += dot_tn(expo, grad)
                if pair == 5:
                    between(2)
            dkey, dvalue = self.r.dkey[...], self.r.dvalue[...]
        else:
            count = 8 * SHORT
            share = s.part[...].reshape(count, 128)
            grad = jnp.concatenate([unpack_one(s.dm_in[index], self.rows) for index in range(8)], 0)
            grad = (grad * share).astype(BF16)
            expo = s.expo[...]
            weighted = expo * dot_nt(grad, s.value[...])
            inner = jnp.sum(weighted, -1, keepdims=True) * share[:, :1]
            draw = (weighted - expo * inner).astype(BF16)
            dq = (dot(draw, s.key[...]) * 0.125).reshape(8, SHORT, 128)
            for index in range(8):
                s.dq_out[index] = self.pack_one(dq[index])
            dkey = dot_tn(draw, s.query[...].reshape(count, 128))
            dvalue = dot_tn(expo, grad)
        self.send(DQ)
        both = jnp.where(own, dkey, pltpu.roll(dvalue, 64, 1)).astype(BF16)
        both = both.reshape(8, 2, self.rows, 128)
        for which in range(2):
            s.dkv_part[which] = both[:, which]

    def _merge(self):
        s = self.s
        return remote(
            s.dkv_part.at[1 - self.at.core], s.dkv_other, s.sems.at[0, 7], s.sems.at[1, 7], self.at.partner()
        )

    def merge_start(self):
        self.at.start(self._merge(), (self.index, 14))

    def merge(self):
        s = self.s
        self.at.finish(self._merge(), (self.index, 14))
        s.dkv_out[...] = (s.dkv_part[self.at.core].astype(F32) + s.dkv_other[...].astype(F32)).astype(BF16)

    def project_back(self):
        i, s, rows = self.index, self.s, self.rows
        cosine, sine = self.angles()
        low = lanes((rows, 128)) < 64
        back = jnp.zeros((rows, D), F32)
        for group in range(GROUPS):
            even, odd = s.dkv_in[2 * group].astype(F32), s.dkv_in[2 * group + 1].astype(F32)
            key = jnp.where(low, even, odd)
            key = key * cosine - half_turn(key) * sine
            value = pltpu.roll(jnp.where(low, odd, even), 64, 1)
            query = unpack_pair(s.dq_in[2 * group], s.dq_in[2 * group + 1], rows)
            query = query * cosine - half_turn(query) * sine
            for which, piece in enumerate((query, key, value)):
                place = 4 * which + group
                column = 128 * (place % 6)
                s.dproj[place // 6, :, column : column + 128] = piece.astype(BF16)
        for part in range(2):
            back = back + dot_nt(s.dproj[part], self.r.wqkv[i, :, 768 * part : 768 * part + 768])
        normal, scale = s.normal[0], s.scale[0][:, :1]
        self.r.gsum[2 * i : 2 * i + 1, :] = jnp.sum(back * normal, 0, keepdims=True)
        return s.dfirst[...] + normalize_back(back, normal, scale, self.gain(0))


    def _swap(self, which):
        s, other = self.s, 1 - self.at.core
        src, dst = (
            (s.glow, s.glow_in), (s.n2, s.n2_in), (s.act.at[other], s.act_in), (s.dhid.at[other], s.dhid_in),
            (s.mixed, s.mixed_in), (s.dv1.at[other], s.dv1_in), (s.n1, s.n1_in), (s.dproj.at[other], s.dproj_in),
        )[which]
        return remote(src, dst, s.sems.at[3, which], s.sems.at[4, which], self.at.partner())

    def swap(self, steps):
        copies = [self._swap(which) for which in steps]
        for copy in copies:
            copy.start()
        self.at.sending += [copy.wait_send for copy in copies]
        self.at.coming[(self.index, 10, steps)] = lambda: [copy.wait_recv() for copy in copies]

    def swapped(self, steps):
        self.at.coming.pop((self.index, 10, steps))()

    def grads_feed(self, total):
        s, core = self.s, self.at.core
        for part in range(4):
            at = slice(256 * part, 256 * part + 256)
            total.put_rows(
                part, dot_tn(s.act[core, :, at], s.glow[...]) + dot_tn(s.act_in[:, at], s.glow_in[...])
            )
        for part in range(2):
            at = slice(512 * part, 512 * part + 512)
            up = dot_tn(s.n2[...], s.dhid[core, :, at]) + dot_tn(s.n2_in[...], s.dhid_in[:, at])
            total.put_columns(4 + 2 * part, up[:, :256])
            total.put_columns(5 + 2 * part, up[:, 256:])
        total.put_columns(8, dot_tn(s.mixed[...], s.dv1[core]) + dot_tn(s.mixed_in[...], s.dv1_in[...]))

    def grads_attention(self, total, first):
        s, core = self.s, self.at.core
        grad = dot_tn(s.n1[...], s.dproj[core]) + dot_tn(s.n1_in[...], s.dproj_in[...])
        for part in range(3):
            total.put_columns(first + part, grad[:, 256 * part : 256 * part + 256])


class Total:
    def __init__(self, at, own, kind, result):
        self.at, self.s, self.kind, self.result = at, own, kind, result
        self.first, self.units = own.first, own.grads.shape[1]
        self.ring = self.units > 1

    def put_rows(self, unit, values):
        values = values.astype(BF16)
        for group in range(4):
            self.s.grads[unit // self.units, unit % self.units, group] = values[
                :, 128 * group : 128 * group + 128
            ].reshape(4, 4, 16, 128)

    def put_columns(self, unit, values):
        values = values.astype(BF16)
        for group in range(2):
            self.s.grads[unit // self.units, unit % self.units, 2 * group : 2 * group + 2] = values[
                :, 128 * group : 128 * group + 128
            ].reshape(2, 4, 4, 16, 128)

    def _full(self, part, *places):
        return self.result.at[(self.at.core, part, pl.ds(self.first, self.units), *places)]

    def _place(self, part, stage, distance=0):
        return lax.rem(self.at.at[ORDERS[part][stage]] + distance, 4)

    def _remote(self, src, dst, part, stage, row, distance):
        sems = self.s.sems
        return remote(src, dst, sems.at[row, 3], sems.at[row, part], self.at.peer(ORDERS[part][stage], distance))

    def _scatter(self, part, stage, distance):
        s = self.s
        src = (s.grads, s.sum1, s.sum2)[stage].at[part, :, self._place(part, stage, distance)]
        dst = (s.part0, s.part1, s.part2)[stage].at[part, distance - 1]
        return self._remote(src, dst, part, stage, stage, distance)

    def _gather(self, part, stage, distance):
        place = self._full(part, *[self._place(part, before) for before in range(stage + 1)])
        return self._remote(place, place, part, stage, 3 + stage, distance)

    def _wait(self, row, part=None):
        s = self.s
        place = (s.part0, s.part1, s.part2, s.part0, s.part1, s.part2, None, None, None, s.hop, s.hop)[row]
        sems = s.sems.at[row]
        if part is None:
            remote(place, place, sems.at[3], sems.at[0], self.at.partner()).wait_send()
        else:
            remote(place.at[part], place.at[part], sems.at[3], sems.at[part], self.at.partner()).wait_recv()

    def _begin(self, copies, row, part):
        for copy in copies:
            copy.start()
        self.at.coming[(self.kind, row, part)] = lambda: self._wait(row, part)
        if part == 2:
            self.at.sending.append(lambda: self._wait(row))

    def _arrive(self, row, part):
        self.at.coming.pop((self.kind, row, part))()

    def _direct(self, make, part, stage, row):
        self._begin([make(part, stage, distance) for distance in (1, 3, 2)], row, part)

    def scatter(self):
        s = self.s
        for part in range(3):
            if not self.ring:
                self._direct(self._scatter, part, 0, 0)
                continue
            opposite = s.grads.at[part, :, self._place(part, 0, 2)]
            copies = [
                self._remote(opposite.at[:, pl.ds(2 * way, 2)], s.hop.at[part, way], part, 0, HOP, distance)
                for way, distance in enumerate((1, 3))
            ]
            self._begin(copies, HOP, part)

    def turn(self):
        s = self.s
        for part in range(3):
            self._arrive(HOP, part)
            copies = []
            for way, distance in enumerate((1, 3)):
                place = self._place(part, 0, distance)
                half = pl.ds(2 * way, 2)
                total = s.grads[part, :, place, half].astype(F32) + s.hop[part, way].astype(F32)
                s.grads[part, :, place, half] = total.astype(BF16)
                copies.append(self._remote(s.grads.at[part, :, place], s.part0.at[part, way], part, 0, 0, distance))
            self._begin(copies, 0, part)

    def scattered(self, stage):
        s = self.s
        for part in range(3):
            self._arrive(stage, part)
            src = (s.grads, s.sum1, s.sum2)[stage]
            got = (s.part0, s.part1, s.part2)[stage]
            total = src[part, :, self._place(part, stage)].astype(F32)
            for index in range(got.shape[1]):
                total = total + got[part, index].astype(F32)
            total = total.astype(BF16)
            if stage == 0:
                s.sum1[part] = total
            elif stage == 1:
                s.sum2[part] = total
            else:
                places = [self._place(part, before) for before in range(3)]
                self.result[(self.at.core, part, pl.ds(self.first, self.units), *places)] = total
            if stage < 2:
                self._direct(self._scatter, part, stage + 1, stage + 1)
            else:
                self._direct(self._gather, part, 2, 5)

    def gathered(self, stage):
        for part in range(3):
            self._arrive(3 + stage, part)
            if stage == 2:
                self._direct(self._gather, part, 1, 4)
            else:
                if self.ring:
                    self._begin([self._gather(part, 0, distance) for distance in (1, 3)], 3, part)
                else:
                    self._direct(self._gather, part, 0, 3)
                self._pass(part, (0,))

    def gather_turn(self):
        s = self.s
        for part in range(3):
            self._arrive(3, part)
            copies = []
            for way, distance in enumerate((1, 3)):
                place = self._full(part, self._place(part, 0, 4 - distance), pl.ds(2 * way, 2))
                copies.append(self._remote(place, place, part, 0, BACK, distance))
            self._begin(copies, BACK, part)
            self._pass(part, (1, 3))

    def gather_done(self):
        for part in range(3):
            self._arrive(BACK if self.ring else 3, part)
            self._pass(part, (2,) if self.ring else (1, 2, 3))

    def _pass(self, part, distances):
        send, recv = self.s.sems.at[6, part], self.s.sems.at[7, part]
        for distance in distances:
            place = self._full(part, self._place(part, 0, distance))
            remote(place, place, send, recv, self.at.partner()).start()
        if 2 in distances:
            whole = self._full(part)
            passed = remote(whole, whole, send, recv, self.at.partner())
            self.at.coming[(self.kind, 6, part)] = passed.wait_recv
            self.at.sending.append(passed.wait_send)


def vmem(**shapes):
    return {name: pltpu.VMEM(shape, kind) for name, (shape, kind) in shapes.items()}


def layer_scratch(index, rows):
    length, half = SEQ * rows, padded(rows)
    message = rows + (NOTE if index == 0 else 0)
    shapes = vmem(
        kv_out=((8, message, 128), BF16), kv_in=((SEQ, message, 128), BF16),
        q_out=((8, half, 128), BF16), q_in=((8, half, 128), BF16),
        dm_out=((8, half, 128), BF16), dm_in=((8, half, 128), BF16),
        mix_out=((8, half, 128), BF16), mix_in=((8, half, 128), BF16),
        dq_out=((8, half, 128), BF16), dq_in=((8, half, 128), BF16),
        dkv_part=((2, 8, rows, 128), BF16), dkv_other=((8, rows, 128), BF16),
        dkv_out=((8, rows, 128), BF16), dkv_in=((8, rows, 128), BF16),
        query=((8, rows, 128), BF16), key=((length, 128), BF16), value=((length, 128), BF16),
        expo=((rows, sum(COUNTS)) if index == 0 else (8 * rows, length), BF16), part=((8, rows, 128), F32),
        normal=((2, rows, D), F32), scale=((2, rows, 128), F32),
        dfirst=((rows, D), F32),
        n1=((rows, D), BF16), n2=((rows, D), BF16), mixed=((rows, D), BF16), glow=((rows, D), BF16),
        act=((2, rows, FF // 2), BF16), dhid=((2, rows, FF // 2), BF16),
        dv1=((2, rows, 256), BF16), dproj=((2, rows, 768), BF16),
        n1_in=((rows, D), BF16), n2_in=((rows, D), BF16), mixed_in=((rows, D), BF16), glow_in=((rows, D), BF16),
        act_in=((rows, FF // 2), BF16), dhid_in=((rows, FF // 2), BF16),
        dv1_in=((rows, 256), BF16), dproj_in=((rows, 768), BF16),
        column=((8, rows, 128), F32), line=((8, length), F32),
    )
    if index:
        shapes.update(vmem(slope=((length, 128), F32)))
    shapes.update(sems=pltpu.SemaphoreType.DMA((5, 8)))
    return shapes


def total_scratch(units):
    ways = 2 if units > 1 else 3
    shapes = vmem(
        hop=((3, 2, units, 2, 4, 16, 128), BF16),
        grads=((3, units, 4, 4, 4, 16, 128), BF16),
        part0=((3, ways, units, 4, 4, 16, 128), BF16), sum1=((3, units, 4, 4, 16, 128), BF16),
        part1=((3, 3, units, 4, 16, 128), BF16), sum2=((3, units, 4, 16, 128), BF16),
        part2=((3, 3, units, 16, 128), BF16),
    )
    shapes.update(sems=pltpu.SemaphoreType.DMA((11, 4)))
    return shapes


def common_scratch():
    shapes = vmem(
        tokens=((LONG, D), BF16), cot=((LONG, D), BF16), seg=((1, LONG), jnp.int32), gains=((2, 2, D), BF16),
        offsets=((2, LONG, 128), F32), firsts=((2, 2 * SEQ, 128), F32),
        wqkv=((2, D, 3 * D), BF16), wout=((2, D, D), BF16),
        wup=((2, D, FF), BF16), wdown=((2, FF, D), BF16),
        dkey=((SEQ * LONG, 128), F32), dvalue=((SEQ * LONG, 128), F32),
        second=((4, LONG + 8, 128), F32), share=((4, SHORT + 8, 128), F32),
        work=((4, LONG, 128), F32), spread=((4, LONG, 128), F32),
        tail=((4, 8, 128), F32), ahead=((4, 8, 128), F32),
        output=((LONG, D), BF16), result=((LONG, D), F32),
        gsum=((8, D), F32), gain_in=((4, 4, 8, D), F32), gain_out=((3, 8, D), F32),
    )
    shapes.update(more=pltpu.SemaphoreType.DMA((41,)))
    return shapes


SPACES = (
    common_scratch(), layer_scratch(0, LONG), layer_scratch(1, SHORT),
    *(total_scratch(units) for units in UNITS),
)


def body(*refs):
    spaces, place = [], 14
    for part in SPACES:
        spaces.append(types.SimpleNamespace(**dict(zip(part, refs[place : place + len(part)]))))
        place += len(part)
    at = Place()
    steps(at, spaces, *refs[:14])
    for wait in at.coming.values():
        wait()
    for wait in at.sending:
        wait()


def steps(
    at, spaces, tokens, seg, wqkv, wout, wup, wdown, gains, cot, offsets, firsts,
    output, tokens_grad, sums, gain_sum,
):
    ref = spaces[0]
    more = ref.more
    full, short = Layer(at, ref, spaces[1], 0, LONG), Layer(at, ref, spaces[2], 1, SHORT)
    for kind in range(3):
        spaces[3 + kind].first = sum(UNITS[:kind])
    early, middle, late = (Total(at, spaces[3 + kind], 20 + kind, sums) for kind in range(3))

    pairs = [
        (tokens, ref.tokens), (gains, ref.gains), (wqkv.at[0], ref.wqkv.at[0]),
        (offsets, ref.offsets), (firsts, ref.firsts), (seg, ref.seg),
        (wout.at[0], ref.wout.at[0]), (wup.at[0], ref.wup.at[0]), (wdown.at[0], ref.wdown.at[0]),
        (wqkv.at[1], ref.wqkv.at[1]), (cot, ref.cot),
        (wout.at[1], ref.wout.at[1]), (wup.at[1], ref.wup.at[1]), (wdown.at[1], ref.wdown.at[1]),
    ]
    loads = [pltpu.make_async_copy(src, dst, more.at[step]) for step, (src, dst) in enumerate(pairs)]
    for load in loads:
        load.start()
    waiting = list(range(len(loads)))

    def loaded(count):
        while waiting and waiting[0] < count:
            loads[waiting.pop(0)].wait()

    at.sending.append(lambda: loaded(len(loads)))
    barrier = pltpu.get_barrier_semaphore()
    greeted = at.greet(barrier)

    loaded(6)
    inputs = ref.tokens[...].astype(F32)
    def ready():
        line = ref.seg[...].astype(F32)
        high = jnp.floor(line * (1.0 / 64.0))
        rows = jnp.concatenate([high, line - 64.0 * high, jnp.zeros((6, LONG), F32)], 0)
        third = jnp.where(sublanes((LONG, 128)) == 3 * lanes((LONG, 128)), 1.0, 0.0)
        picked = dot(rows, third)
        wide = jnp.concatenate([rows[:, 128:], jnp.zeros((8, 112), F32)], 1)
        note = jnp.concatenate([rows[0:2, :128], wide[0:2], picked[0:2], jnp.zeros((10, 128), F32)], 0)
        for head in range(8):
            full.s.kv_out[head, LONG:] = note.astype(BF16)
        pl.semaphore_wait(barrier, greeted)

    full.project(inputs, ready)

    def segments():
        notes = [full.s.kv_in[block, LONG:, :].astype(F32) for block in range(SEQ)]
        for block, code in enumerate(notes):
            long = jnp.concatenate([64.0 * code[0:1] + code[1:2], 64.0 * code[2:3, :16] + code[3:4, :16]], 1)
            full.s.line[0:1, LONG * block : LONG * block + LONG] = long
            short.s.line[0:1, SHORT * block : SHORT * block + SHORT] = (64.0 * code[4:5] + code[5:6])[:, :SHORT]
        for layer in (full, short):
            rows = layer.rows
            equal = lanes((rows, rows)) == sublanes((rows, rows))
            for pair in range(8):
                code = full.s.kv_in[2 * pair + at.core, LONG:, :].astype(F32)
                if layer is full:
                    line = jnp.concatenate([64.0 * code[0:1] + code[1:2], 64.0 * code[2:3, :16] + code[3:4, :16]], 1)
                else:
                    line = (64.0 * code[4:5] + code[5:6])[:, :SHORT]
                column = jnp.sum(jnp.where(equal, line, 0.0), 1, keepdims=True)
                layer.s.column[pair] = jnp.broadcast_to(column, (rows, 128))

    def attention(layer):
        layer.receive_keys()
        layer.receive(Q)
        if layer is full:
            segments()
        layer.split_heads()
        layer.attend()
        layer.receive(MIX)

    attention(full)
    loaded(9)
    second = ref.second
    spill(second, 8, full.feed_forward(inputs))

    def halo():
        return remote(second.at[:, pl.ds(LONG, 8), :], ref.tail, more.at[17], more.at[18], at.along(1))

    at.start(halo(), (3, 0))
    loaded(11)
    work = ref.work
    spill(work, 0, ref.cot[...].astype(F32))
    grad_short = jnp.concatenate(
        [every_third(work, 0, g) + every_third(work, 1, g) + every_third(work, 2, g) for g in range(GROUPS)], 1
    )
    at.finish(halo(), (3, 0))
    second[:, 0:8, :] = jnp.where(at.seq == 0, 0.0, ref.tail[...])
    pooled = jnp.concatenate(
        [
            (every_third(second, 6, g) + every_third(second, 7, g) + every_third(second, 8, g)) / 3.0
            for g in range(GROUPS)
        ],
        1,
    )
    short.project(pooled)
    loaded(14)
    attention(short)
    result = short.feed_forward(pooled)

    def backward(layer, total, grad, between):
        layer.feed_back(grad)
        layer.swap(SEVEN)
        between(0)
        layer.swapped(SEVEN)
        layer.grads_feed(total)
        between(1)
        layer.receive(DM)
        layer.attend_back(between)
        layer.merge_start()
        between(3)
        layer.merge()
        layer.send(DKV)
        between(4)
        layer.receive(DQ)
        layer.receive(DKV)
        back = layer.project_back()
        layer.swap((7,))
        return back

    spread = ref.spread

    def finish_output():
        for group in range(GROUPS):
            at_lanes = slice(128 * group, 128 * group + 128)
            for step in range(3):
                spread[group, pl.ds(step, SHORT, 3), :] = every_third(second, 8 + step, group) + result[:, at_lanes]
            ref.output[:, at_lanes] = spread[group].astype(BF16)
        store = pltpu.make_async_copy(ref.output, output, more.at[14])
        store.start()
        at.sending.append(store.wait)

    def between_short(point):
        if point == 0:
            finish_output()
        elif point == 4:
            early.scatter()

    share = ref.share
    spill(share, 0, backward(short, early, grad_short, between_short) * (1.0 / 3.0))

    def halo_back():
        return remote(share.at[:, pl.ds(0, 8), :], ref.ahead, more.at[19], more.at[20], at.along(SEQ - 1))

    at.start(halo_back(), (3, 1))
    early.turn()
    short.swapped((7,))
    short.grads_attention(middle, 9)
    at.finish(halo_back(), (3, 1))
    share[:, SHORT:, :] = jnp.where(at.seq == SEQ - 1, 0.0, ref.ahead[...])
    for group in range(GROUPS):
        own, following = share[group, 0:SHORT, :], share[group, 1 : SHORT + 1, :]
        for step, piece in enumerate((own, following, following)):
            spread[group, pl.ds(step, SHORT, 3), :] = every_third(work, step, group) + piece
    grad_full = jnp.concatenate([spread[group] for group in range(GROUPS)], 1)

    def between_full(point):
        if point == 0:
            early.scattered(0)
        elif point == 1:
            middle.scatter()
            early.scattered(1)
        elif point == 2:
            early.scattered(2)
            middle.turn()
        elif point == 3:
            early.gathered(2)
        else:
            middle.scattered(0)
            early.gathered(1)

    ref.result[...] = backward(full, middle, grad_full, between_full)
    store = pltpu.make_async_copy(ref.result, tokens_grad, more.at[15])
    store.start()
    at.sending.append(store.wait)
    middle.scattered(1)
    full.swapped((7,))
    full.grads_attention(late, 0)
    late.scatter()

    gsum, gain_in, gain_out = ref.gsum, ref.gain_in, ref.gain_out

    def gain_copy(axis, distance):
        src = gsum if axis == 0 else gain_out.at[axis - 1]
        return remote(
            src, gain_in.at[axis, at.at[axis]], more.at[22 + 3 * axis + distance], more.at[31 + 3 * axis + distance],
            at.peer(axis, distance),
        )

    def gain_step(axis):
        for distance in (1, 2, 3):
            at.start(gain_copy(axis, distance), (4, axis, distance))
        gain_in[axis, at.at[axis]] = gsum[...] if axis == 0 else gain_out[axis - 1]

    def gain_done(axis):
        for distance in (1, 2, 3):
            at.finish(gain_copy(axis, distance), (4, axis, distance))
        return (gain_in[axis, 0] + gain_in[axis, 1]) + (gain_in[axis, 2] + gain_in[axis, 3])

    gsum[4:, :] = jnp.zeros((4, D), F32)
    gain_step(0)
    early.gather_turn()
    middle.scattered(2)
    late.scattered(0)
    gain_out[0] = gain_done(0)
    gain_step(1)
    middle.gathered(2)
    late.scattered(1)
    gain_out[1] = gain_done(1)
    gain_step(2)
    early.gather_done()
    late.scattered(2)
    middle.gathered(1)
    late.gathered(2)
    middle.gather_turn()
    late.gathered(1)
    gain_in[3, 0] = gain_done(2)
    gain_swap = remote(gain_in.at[3, 0], gain_in.at[3, 1], more.at[21], more.at[22], at.partner())
    at.start(gain_swap, (4, 3, 0))
    middle.gather_done()
    late.gather_done()
    at.finish(gain_swap, (4, 3, 0))
    gain_out[2] = gain_in[3, 0] + gain_in[3, 1]
    store = pltpu.make_async_copy(gain_out.at[2], gain_sum, more.at[16])
    store.start()
    at.sending.append(store.wait)


def tables():
    freq = 10000.0 ** (-np.arange(32) / 32.0)
    freq = np.tile(freq, 4)[None, :]
    offset = np.arange(LONG)[:, None] * freq
    first = np.concatenate([np.arange(SEQ) * LONG, np.arange(SEQ) * SHORT])[:, None] * freq
    return (
        np.stack([np.cos(offset), np.sin(offset)]).astype(np.float32),
        np.stack([np.cos(first), np.sin(first)]).astype(np.float32),
    )


def widen_body(
    sums, gain, output, grad, qkv, out, up, down, gains, output_too, grad_too,
    gain_in, gain_out, output_in, grad_in, down_out, up_out, out_out, qkv_out, sems,
):
    small = [
        pltpu.make_async_copy(gain, gain_in, sems.at[0, 0]),
        pltpu.make_async_copy(output, output_in, sems.at[0, 1]),
        pltpu.make_async_copy(grad, grad_in, sems.at[0, 2]),
    ]
    stores = []
    for copy in small:
        copy.start()

    def put(dst, src, slot):
        copy = pltpu.make_async_copy(src, dst, sems.at[1 + slot // 8, slot % 8])
        copy.start()
        stores.append(copy)

    def tiles(kind, half, unit):
        return sums.at[half, unit // UNITS[kind], sum(UNITS[:kind]) + unit % UNITS[kind]]

    def rows_of(kind, half, unit, dst, first_row):
        ref = tiles(kind, half, unit)
        for group in range(4):
            values = ref[group].reshape(256, 128).astype(F32)
            dst[first_row : first_row + 256, 128 * group : 128 * group + 128] = values

    def columns_of(kind, half, unit, dst, column):
        ref = tiles(kind, half, unit)
        for group in range(2):
            values = ref[2 * group : 2 * group + 2].reshape(512, 128).astype(F32)
            dst[:, column + 128 * group : column + 128 * group + 128] = values

    def feed(kind, half, block):
        at = 2 * block + half
        for unit in range(4):
            rows_of(kind, half, unit, down_out.at[at], 256 * unit)
        put(down.at[block, pl.ds(1024 * half, 1024), :], down_out.at[at], at)

    def rest(kind, block, kind_heads, unit):
        for half in range(2):
            for part in range(4):
                columns_of(kind, half, 4 + part, up_out.at[block], 1024 * half + 256 * part)
        put(up.at[block], up_out.at[block], 4 + block)
        for half in range(2):
            columns_of(kind, half, 8, out_out.at[block], 256 * half)
        put(out.at[block], out_out.at[block], 6 + block)
        for half in range(2):
            for part in range(3):
                columns_of(kind_heads, half, unit + part, qkv_out.at[block], 768 * half + 256 * part)
        put(qkv.at[block], qkv_out.at[block], 8 + block)

    def through():
        for copy in small:
            copy.wait()
        gain_out[...] = gain_in[0:4, :].reshape(2, 2, D)
        put(gains, gain_out, 10)
        put(output_too.at[0], output_in, 11)
        put(grad_too.at[0], grad_in, 12)

    for kind, block, kind_heads, unit in ((0, 1, 1, 9), (1, 0, 2, 0)):
        for half in range(2):
            feed(kind, half, block)
        rest(kind, block, kind_heads, unit)
        if kind == 0:
            through()
    for copy in stores:
        copy.wait()


def widen(sums, gain, output, grad):
    anywhere, inside = pl.BlockSpec(memory_space=pl.ANY), pl.BlockSpec(memory_space=pltpu.VMEM)
    return pl.pallas_call(
        widen_body,
        out_shape=(
            jax.ShapeDtypeStruct((2, D, 3 * D), F32),
            jax.ShapeDtypeStruct((2, D, D), F32),
            jax.ShapeDtypeStruct((2, D, FF), F32),
            jax.ShapeDtypeStruct((2, FF, D), F32),
            jax.ShapeDtypeStruct((2, 2, D), F32),
            jax.ShapeDtypeStruct((1, LONG, D), BF16),
            jax.ShapeDtypeStruct((1, LONG, D), F32),
        ),
        in_specs=[inside] + [anywhere] * 3,
        out_specs=(anywhere,) * 7,
        scratch_shapes=[
            pltpu.VMEM((8, D), F32),
            pltpu.VMEM((2, 2, D), F32),
            pltpu.VMEM((LONG, D), BF16),
            pltpu.VMEM((LONG, D), F32),
            pltpu.VMEM((4, 1024, 512), F32),
            pltpu.VMEM((2, 512, 2048), F32),
            pltpu.VMEM((2, 512, 512), F32),
            pltpu.VMEM((2, 512, 1536), F32),
            pltpu.SemaphoreType.DMA((3, 8)),
        ],
        compiler_params=pltpu.CompilerParams(vmem_limit_bytes=40 * 2**20),
        name="widen",
    )(
        pltpu.with_memory_space_constraint(sums, pltpu.VMEM),
        *(pltpu.with_memory_space_constraint(array, pltpu.HBM) for array in (gain, output, grad)),
    )


def per_device(tokens, segment, w_qkv, w_out, w_up, w_down, gains, cotangent):
    offsets, firsts = tables()
    anywhere, inside = pl.BlockSpec(memory_space=pl.ANY), pl.BlockSpec(memory_space=pltpu.VMEM)
    output, tokens_grad, sums, gain = pl.pallas_call(
        body,
        out_shape=(
            jax.ShapeDtypeStruct((LONG, D), BF16),
            jax.ShapeDtypeStruct((LONG, D), F32),
            pltpu.VMEM((2, 3, sum(UNITS), 4, 4, 4, 16, 128), BF16),
            jax.ShapeDtypeStruct((8, D), F32),
        ),
        in_specs=[anywhere] * 10,
        out_specs=(anywhere, anywhere, inside, anywhere),
        scratch_shapes=[shape for part in SPACES for shape in part.values()],
        compiler_params=pltpu.CompilerParams(
            collective_id=0, has_side_effects=True, vmem_limit_bytes=51 * 2**20
        ),
        name="layers",
    )(
        tokens[0], segment, w_qkv, w_out, w_up, w_down, gains, cotangent[0],
        jnp.asarray(offsets), jnp.asarray(firsts),
    )
    qkv, out, up, down, gain, output, tokens_grad = widen(sums, gain, output, tokens_grad)
    return output, tokens_grad, qkv, out, up, down, gain


def solution(mesh):
    return jax.shard_map(
        per_device,
        mesh=mesh,
        in_specs=(
            P("row", "seq", None),
            P("row", "seq"),
            P(),
            P(),
            P(),
            P(),
            P(),
            P("row", "seq", None),
        ),
        out_specs=(P("row", "seq", None), P("row", "seq", None), P(), P(), P(), P(), P()),
        check_vma=False,
    )
```

time: 172 us -> 144 us (0.84)
  Pallas kernels: 171 us -> 143 us
    pallas_call x1, Pallas kernels: 156 us -> 134 us  [per_device(): pl.pallas_call(body, out_shape=(jax.ShapeDtypeStruct((LONG, D), BF16), ja...]
    pallas_call x1, Pallas kernels: 14.8 us -> 9 us  [widen(): pl.pallas_call(widen_body, out_shape=(jax.ShapeDtypeStruct((2, D, 3 * D),...]
where the time goes in v2:
time: 144 us
  Pallas kernels  143 us (99%)
    pallas_call x1, Pallas kernels, per_device(): pl.pallas_call(body, out_shape=(jax.ShapeDtypeStruct((LONG, D), BF16), ja...  134 us
    pallas_call x1, Pallas kernels, widen(): pl.pallas_call(widen_body, out_shape=(jax.ShapeDtypeStruct((2, D, 3 * D),...  9 us

profile of v2, /device:TPU:1, one launch (start us, length us, event | category | flops | bytes accessed | tf_op | source)
XLA Modules:
  0.0 144.2 jit_solution(11817880271626362541)
XLA Ops:
  0.6 134.4 %layers.1 = (bf16[144,512]{1,0:T(8,128)(2,1)}, f32[144,512]{1,0:T(8,128)}, bf16[2,3,8,4,4,4,16,128]{7,6,5,4,3,2,1,0:T(8,128)(2,1)S(1)}, f32[8,512]{1,0:T(8,128)}) custom-call(bf16[144,512]{1,0:T(8,128)(2,1)} %bitcast.2, s32[1,144]{1,0:T(1,128)} %refs_1_.1, bf16[2,512,1536]{2,1,0:T(8,128)(2,1)} %refs_2_.1, bf16[2,512,512]{2,1,0:T(8,128)(2,1)} %refs_3_.1, ...), custom_call_target="tpu_custom_call" | custom-call | tf_op jit(solution)/shard_map/layers/pallas_call | solution.py:1115
  135.0 9.0 %widen.1 = (f32[2,512,1536]{2,1,0:T(8,128)}, f32[2,512,512]{2,1,0:T(8,128)}, f32[2,512,2048]{2,1,0:T(8,128)}, f32[2,2048,512]{2,1,0:T(8,128)}, f32[2,2,512]{2,1,...) custom-call(bf16[2,3,8,4,4,4,16,128]{7,6,5,4,3,2,1,0:T(8,128)(2,1)S(1)} %get-tuple-element.18.sums, ...), custom_call_target="tpu_custom_call" | custom-call | tf_op jit(solution)/shard_map/widen/pallas_call | solution.py:1080

commit v3 on v2

--- a/solution.py
+++ b/solution.py
@@ -19,10 +19,11 @@
 FF = 2048
 GROUPS = 4
 NOTE = 16
-KV, Q, DM, MIX, DKV, DQ = range(6)
-SEVEN = tuple(range(7))
-UNITS = (3, 4, 1)
-HOP, BACK = 9, 10
+KV, Q, DM, MIX, DKV, DQ, RELAY, TAIL, MERGE = range(9)
+AHEAD, BEHIND = (1, 2, 4, 6), (0, 3, 5)
+EXTRA = 16
+UNITS = (3, 3, 1, 1)
+HOP, BACK = 7, 8
 X, Y, Z = range(3)
 ORDERS = ((X, Y, Z), (Y, Z, X), (Z, X, Y))
 
@@ -117,7 +118,9 @@
         self.core = lax.rem(self.row, 2)
         self.at = (self.row // 2, lax.rem(self.seq, 4), self.seq // 4)
         self.head = lax.rem(self.seq, 8)
-        self.same = (self.seq // 8 == self.core) & (lax.rem(self.seq, 2) == self.core)
+        self.near = self.seq // 8 == self.core
+        odd = lax.rem(self.seq, 2)
+        self.same, self.next = self.near & (odd == self.core), self.near & (odd != self.core)
         self.sending, self.coming = [], {}
 
     def peer(self, axis, distance):
@@ -134,13 +137,14 @@
     def along(self, distance):
         return (self.row, lax.rem(self.seq + distance, SEQ))
 
-    def holder(self, head):
-        device = (2 * self.at[X] + lax.rem(self.seq, 2), 8 * self.core + head)
-        return device, self.same & (self.head == head)
-
-    def owner(self, index):
-        device = (2 * self.at[X] + self.seq // 8, 2 * index + self.core)
-        return device, self.same & (self.seq // 2 == index)
+    def _with_same(self, row, seq):
+        return (row, seq), (row == self.row) & (seq == self.seq)
+
+    def holder(self, head, core):
+        return self._with_same(2 * self.at[X] + core, 8 * self.core + head)
+
+    def owner(self, stretch):
+        return self._with_same(2 * self.at[X] + self.seq // 8, stretch)
 
     def start(self, copy, key):
         copy.start()
@@ -152,19 +156,21 @@
         copy.wait_recv()
 
     def greet(self, barrier):
-        for make in (self.holder, self.owner):
-            for index in range(8):
-                device, same = make(index)
+        def one(index, carry):
+            for device, same in (self.holder(index // 2, lax.rem(index, 2)), self.owner(index)):
 
                 @pl.when(jnp.logical_not(same))
                 def _():
                     pl.semaphore_signal(barrier, inc=1, device_id=device, device_id_type=MESH)
 
+            return carry
+
+        lax.fori_loop(0, 16, one, 0)
         others = [self.partner(), self.along(1), self.along(SEQ - 1)]
         others += [self.peer(axis, distance) for axis in (X, Y, Z) for distance in (1, 2, 3)]
         for device in others:
             pl.semaphore_signal(barrier, inc=1, device_id=device, device_id_type=MESH)
-        return 16 + len(others) - 2 * self.same.astype(jnp.int32)
+        return 32 + len(others) - 2 * self.near.astype(jnp.int32)
 
 
 COUNTS = [-(-2 * LONG * (pair + 1) // 128) * 128 for pair in range(8)]
@@ -178,27 +184,40 @@
         self.s = own
         self.index = index
         self.rows = rows
-        self.slope = own.slope if index else ref.dkey
+        self.slope = ref.dvalue if index else ref.dkey
 
 
     def _buffers(self, kind):
         s = self.s
-        return (
-            (s.kv_out, s.kv_in), (s.q_out, s.q_in), (s.dm_out, s.dm_in),
-            (s.mix_out, s.mix_in), (s.dkv_out, s.dkv_in), (s.dq_out, s.dq_in),
-        )[kind]
+        return {
+            KV: (s.kv_out, s.kv_in), Q: (s.q_out, s.q_in), DM: (s.dm_out, s.dm_in), MIX: (s.mix_out, s.mix_in),
+            DKV: (s.dkv_out, s.dkv_in), DQ: (s.dq_out, s.dq_in), TAIL: (self.r.tail_out, self.r.tail_in),
+        }[kind]
+
+    def _wide(self, kind):
+        return self.index == 1 and kind in (KV, DKV)
 
     def _copy(self, kind, index):
         at, sems = self.at, self.s.sems
         out, into = self._buffers(kind)
+        source, recv = index, sems.at[1, kind]
         if kind in (KV, Q, DM):
-            (device, same), slot = at.holder(index), at.seq // 2
-            target = at.seq if kind == KV else slot
+            if self._wide(kind):
+                source = index // 2
+                device, same = at.holder(source, lax.rem(index, 2))
+            else:
+                device, same = at.holder(index, lax.rem(at.seq, 2))
+            target = at.seq if kind == KV else at.seq // 2
+            if kind == KV and not self._wide(kind):
+                recv = sems.at[2, at.seq // 2]
+            into = into.at[target]
+        elif self._wide(kind):
+            device, same = at.owner(index)
+            into = into.at[at.core, at.head]
         else:
-            (device, same), slot = at.owner(index), at.head
-            target = slot
-        recv = sems.at[2, slot] if kind == KV else sems.at[1, kind]
-        return out.at[index], into.at[target], sems.at[0, kind], recv, device, same
+            device, same = at.owner(lax.rem(2 * index + at.core + (1 if kind == TAIL else 0), SEQ))
+            into = into.at[at.head]
+        return out.at[source], into, sems.at[0, kind], recv, device, same
 
     def send_one(self, kind, index):
         src, dst, send, recv, device, same = self._copy(kind, index)
@@ -211,18 +230,30 @@
         def _():
             remote(src, dst, send, recv, device).start()
 
+    def send_some(self, kind, first):
+        def one(step, carry):
+            index = lax.rem(step + self.at.head, 4) + first
+            self.send_one(kind, index)
+            if kind == MIX:
+                self.send_one(TAIL, index)
+            return carry
+
+        lax.fori_loop(0, 4, one, 0)
+
     def send_rest(self, kind):
         self.at.sending.append(lambda: self.sent(kind))
         self.at.coming[(self.index, kind)] = lambda: self.receive(kind)
 
     def send(self, kind):
+        count = 16 if self._wide(kind) else 8
         begin = self.at.seq // 2 if kind in (KV, Q, DM) else self.at.head
+        begin = begin * (count // 8)
 
         def one(step, carry):
-            self.send_one(kind, lax.rem(step + begin, 8))
+            self.send_one(kind, lax.rem(step + begin, count))
             return carry
 
-        lax.fori_loop(0, 8, one, 0)
+        lax.fori_loop(0, count, one, 0)
         self.send_rest(kind)
 
     def _wait(self, place, send, recv):
@@ -234,22 +265,25 @@
         self._wait(self._buffers(kind)[1], sems.at[0, kind], sems.at[1, kind]).wait_recv()
 
     def sent(self, kind):
-        out, sems = self._buffers(kind)[0], self.s.sems
-
-        @pl.when(self.at.same)
-        def _():
-            self._wait(out.at[pl.ds(0, 7)], sems.at[0, kind], sems.at[1, kind]).wait_send()
-
-        @pl.when(jnp.logical_not(self.at.same))
-        def _():
-            self._wait(out, sems.at[0, kind], sems.at[1, kind]).wait_send()
+        sems = self.s.sems
+        count = 16 if self._wide(kind) else 8
+        many = self.s.kv_in if kind == KV else self._buffers(kind)[0]
+        inside = self.at.near if self._wide(kind) else self.at.next if kind == TAIL else self.at.same
+        for number, when in ((count - 1, inside), (count, jnp.logical_not(inside))):
+
+            @pl.when(when)
+            def _():
+                self._wait(many.at[pl.ds(0, number)], sems.at[0, kind], sems.at[1, kind]).wait_send()
 
     def _relay(self, index):
         place = self.s.kv_in.at[2 * index + self.at.core]
         sems = self.s.sems
-        return remote(place, place, sems.at[0, 6], sems.at[1, 6], self.at.partner())
+        return remote(place, place, sems.at[0, RELAY], sems.at[1, RELAY], self.at.partner())
 
     def receive_keys(self):
+        if self._wide(KV):
+            self.receive(KV)
+            return
         self.at.coming.pop((self.index, KV), None)
         s = self.s
 
@@ -259,7 +293,7 @@
             return carry
 
         lax.fori_loop(0, 8, one, 0)
-        relayed = self._wait(s.kv_in.at[pl.ds(0, 8)], s.sems.at[0, 6], s.sems.at[1, 6])
+        relayed = self._wait(s.kv_in.at[pl.ds(0, 8)], s.sems.at[0, RELAY], s.sems.at[1, RELAY])
         relayed.wait_recv()
         self.at.sending.append(relayed.wait_send)
 
@@ -322,7 +356,7 @@
                 count = COUNTS[pair]
                 score = dot_nt(s.query[pair], s.key[:count])
                 first = (288 * pair) // 128 * 128
-                column = s.column[pair][:, :1]
+                column = s.column[:, pair : pair + 1]
                 allowed = s.line[0:1, :count] == column
                 position = sublanes((LONG, count - first)) + (2 * pair + core) * LONG
                 causal = lanes((LONG, count - first)) + first <= position
@@ -337,10 +371,16 @@
                 share = 1.0 / jnp.sum(expo, -1, keepdims=True)
                 expo = expo.astype(BF16)
                 s.expo[:, FIRSTS[pair] : FIRSTS[pair] + count] = expo
-                s.part[pair] = jnp.broadcast_to(share, (LONG, 128))
-                s.mix_out[pair] = self.pack_one(dot(expo, s.value[:count]) * share)
-                self.send_one(MIX, pair)
+                s.part[:, pair : pair + 1] = share
+                mixed = dot(expo, s.value[:count]) * share
+                s.mix_out[pair] = self.pack_one(mixed)
+                tail = mixed[LONG - EXTRA :]
+                self.r.tail_out[pair] = jnp.where(self.native(tail.shape), tail, 0.0).astype(BF16)
+                if pair == 4:
+                    self.send_some(MIX, 4)
+            self.send_some(MIX, 0)
             self.send_rest(MIX)
+            self.send_rest(TAIL)
         else:
             count, length = 8 * SHORT, SEQ * SHORT
             score = dot_nt(s.query[...].reshape(count, 128), s.key[...])
@@ -362,16 +402,19 @@
             self.send(MIX)
 
     def feed_forward(self, values):
-        i, s = self.index, self.s
-        parts = [unpack_pair(s.mix_in[2 * g], s.mix_in[2 * g + 1], self.rows) for g in range(GROUPS)]
+        i, s, rows = self.index, self.s, self.rows
+        parts = [unpack_pair(s.mix_in[2 * g], s.mix_in[2 * g + 1], rows) for g in range(GROUPS)]
         mixed = jnp.concatenate(parts, 1).astype(BF16)
         s.mixed[...] = mixed
+        if i == 0:
+            tails = [self.r.tail_in[2 * g] + self.r.tail_in[2 * g + 1] for g in range(GROUPS)]
+            mixed = jnp.concatenate([mixed, jnp.concatenate(tails, 1)], 0)
         first = values + dot(mixed, self.r.wout[i])
         normal, scale = normalize(first)
-        s.normal[1] = normal
-        s.scale[1] = jnp.broadcast_to(scale, (self.rows, 128))
+        s.normal[1] = normal[:rows]
+        s.scale[1] = jnp.broadcast_to(scale[:rows], (rows, 128))
         normed = (normal * self.gain(1)).astype(BF16)
-        s.n2[...] = normed
+        s.n2[...] = normed[:rows]
         result = first
         for part in range(4):
             at = slice(512 * part, 512 * part + 512)
@@ -379,14 +422,15 @@
             inner = 0.7978845608028654 * (hidden + 0.044715 * hidden * hidden * hidden)
             bend = jnp.tanh(inner)
             active = (0.5 * hidden * (1.0 + bend)).astype(BF16)
+            result = result + dot(active, self.r.wdown[i, at, :])
+            s.act[part // 2, :, 512 * (part % 2) : 512 * (part % 2) + 512] = active[:rows]
+            hidden, bend = hidden[:rows], bend[:rows]
             slope = 0.5 * (1.0 + bend) + 0.5 * hidden * (1.0 - bend * bend) * (
                 0.7978845608028654 * (1.0 + 3.0 * 0.044715 * hidden * hidden)
             )
             for column in range(4):
-                place = self.rows * (4 * part + column)
-                self.slope[place : place + self.rows, :] = slope[:, 128 * column : 128 * column + 128]
-            s.act[part // 2, :, 512 * (part % 2) : 512 * (part % 2) + 512] = active
-            result = result + dot(active, self.r.wdown[i, at, :])
+                place = rows * (4 * part + column)
+                self.slope[place : place + rows, :] = slope[:, 128 * column : 128 * column + 128]
         return result
 
 
@@ -394,6 +438,7 @@
         i, s = self.index, self.s
         low = grad.astype(BF16)
         s.glow[...] = low
+        self.swap((0,))
         back = jnp.zeros((self.rows, D), F32)
         for part in range(4):
             at = slice(512 * part, 512 * part + 512)
@@ -403,6 +448,7 @@
             hidden = (slope * active).astype(BF16)
             s.dhid[part // 2, :, 512 * (part % 2) : 512 * (part % 2) + 512] = hidden
             back = back + dot_nt(hidden, self.r.wup[i, :, at])
+        self.swap((3,))
         normal, scale = s.normal[1], s.scale[1][:, :1]
         self.r.gsum[2 * i + 1 : 2 * i + 2, :] = jnp.sum(back * normal, 0, keepdims=True)
         first = grad + normalize_back(back, normal, scale, self.gain(1))
@@ -410,6 +456,7 @@
         first_low = first.astype(BF16)
         s.dv1[0] = first_low[:, :256]
         s.dv1[1] = first_low[:, 256:]
+        self.swap((5,))
         for group in range(GROUPS):
             weight = self.r.wout[i, 128 * group : 128 * group + 128, :]
             s.dm_out[2 * group], s.dm_out[2 * group + 1] = pack_pair(dot_nt(first_low, weight))
@@ -419,22 +466,30 @@
         s, length = self.s, SEQ * self.rows
         own = self.native((length, 128))
         if self.index == 0:
-            self.r.dkey[...] = jnp.zeros((length, 128), F32)
-            self.r.dvalue[...] = jnp.zeros((length, 128), F32)
             for pair in reversed(range(8)):
                 count = COUNTS[pair]
-                share = s.part[pair]
+                share = s.part[:, pair : pair + 1]
                 grad = (unpack_one(s.dm_in[pair], self.rows) * share).astype(BF16)
                 expo = s.expo[:, FIRSTS[pair] : FIRSTS[pair] + count]
                 weighted = expo * dot_nt(grad, s.value[:count])
-                inner = jnp.sum(weighted, -1, keepdims=True) * share[:, :1]
+                inner = jnp.sum(weighted, -1, keepdims=True) * share
                 draw = (weighted - expo * inner).astype(BF16)
                 s.dq_out[pair] = self.pack_one(dot(draw, s.key[:count]) * 0.125)
-                self.r.dkey[:count] += dot_tn(draw, s.query[pair])
-                self.r.dvalue[:count] += dot_tn(expo, grad)
-                if pair == 5:
-                    between(2)
-            dkey, dvalue = self.r.dkey[...], self.r.dvalue[...]
+                for total, left, right in ((self.r.dkey, draw, s.query[pair]), (self.r.dvalue, expo, grad)):
+                    if pair == 7:
+                        total[...] = dot_tn(left, right)
+                    else:
+                        total[:count] += dot_tn(left, right)
+                if pair == 4:
+                    self.part_done(1)
+                    self.send_some(DQ, 4)
+                if pair == 1:
+                    self.merge(1)
+                between(10 + pair)
+            self.part_done(0)
+            self.send_some(DQ, 0)
+            self.send_rest(DQ)
+            return
         else:
             count = 8 * SHORT
             share = s.part[...].reshape(count, 128)
@@ -451,23 +506,28 @@
             dvalue = dot_tn(expo, grad)
         self.send(DQ)
         both = jnp.where(own, dkey, pltpu.roll(dvalue, 64, 1)).astype(BF16)
-        both = both.reshape(8, 2, self.rows, 128)
+        s.dkv_out[...] = both.reshape(SEQ, self.rows, 128)
+
+    def part_done(self, half):
+        s, rows = self.s, SEQ * self.rows // 2
+        place = slice(rows * half, rows * half + rows)
+        value = pltpu.roll(self.r.dvalue[place], 64, 1)
+        both = jnp.where(self.native((rows, 128)), self.r.dkey[place], value).astype(BF16)
+        both = both.reshape(4, 2, self.rows, 128)
         for which in range(2):
-            s.dkv_part[which] = both[:, which]
-
-    def _merge(self):
-        s = self.s
-        return remote(
-            s.dkv_part.at[1 - self.at.core], s.dkv_other, s.sems.at[0, 7], s.sems.at[1, 7], self.at.partner()
-        )
-
-    def merge_start(self):
-        self.at.start(self._merge(), (self.index, 14))
-
-    def merge(self):
-        s = self.s
-        self.at.finish(self._merge(), (self.index, 14))
-        s.dkv_out[...] = (s.dkv_part[self.at.core].astype(F32) + s.dkv_other[...].astype(F32)).astype(BF16)
+            s.dkv_part[which, 4 * half : 4 * half + 4] = both[:, which]
+        self.at.start(self._merge(half), (self.index, 14, half))
+
+    def _merge(self, half):
+        s, four = self.s, pl.ds(4 * half, 4)
+        send, recv = s.sems.at[0, MERGE + half], s.sems.at[1, MERGE + half]
+        return remote(s.dkv_part.at[1 - self.at.core, four], s.dkv_other.at[four], send, recv, self.at.partner())
+
+    def merge(self, half):
+        s, four = self.s, slice(4 * half, 4 * half + 4)
+        self.at.finish(self._merge(half), (self.index, 14, half))
+        s.dkv_out[four] = (s.dkv_part[self.at.core, four].astype(F32) + s.dkv_other[four].astype(F32)).astype(BF16)
+        self.send_some(DKV, 4 * half)
 
     def project_back(self):
         i, s, rows = self.index, self.s, self.rows
@@ -475,7 +535,13 @@
         low = lanes((rows, 128)) < 64
         back = jnp.zeros((rows, D), F32)
         for group in range(GROUPS):
-            even, odd = s.dkv_in[2 * group].astype(F32), s.dkv_in[2 * group + 1].astype(F32)
+            if i:
+                even, odd = (
+                    s.dkv_in[0, head].astype(F32) + s.dkv_in[1, head].astype(F32)
+                    for head in (2 * group, 2 * group + 1)
+                )
+            else:
+                even, odd = s.dkv_in[2 * group].astype(F32), s.dkv_in[2 * group + 1].astype(F32)
             key = jnp.where(low, even, odd)
             key = key * cosine - half_turn(key) * sine
             value = pltpu.roll(jnp.where(low, odd, even), 64, 1)
@@ -536,6 +602,7 @@
         self.at, self.s, self.kind, self.result = at, own, kind, result
         self.first, self.units = own.first, own.grads.shape[1]
         self.ring = self.units > 1
+        self.spread = (self.units, self.units + 1, 0, self.units)[kind - 20]
 
     def put_rows(self, unit, values):
         values = values.astype(BF16)
@@ -551,19 +618,24 @@
                 :, 128 * group : 128 * group + 128
             ].reshape(2, 4, 4, 16, 128)
 
-    def _full(self, part, *places):
-        return self.result.at[(self.at.core, part, pl.ds(self.first, self.units), *places)]
+    def _full(self, *places):
+        if not places:
+            places = (slice(None),)
+        return self.result.at[(self.at.core, places[0], pl.ds(self.first, self.spread), *places[1:])]
 
     def _place(self, part, stage, distance=0):
         return lax.rem(self.at.at[ORDERS[part][stage]] + distance, 4)
 
+    def _mine(self, part, count):
+        return [self._place(part, before) for before in range(count)]
+
     def _remote(self, src, dst, part, stage, row, distance):
         sems = self.s.sems
-        return remote(src, dst, sems.at[row, 3], sems.at[row, part], self.at.peer(ORDERS[part][stage], distance))
+        return remote(src, dst, sems.at[row, 0], sems.at[row, 1], self.at.peer(ORDERS[part][stage], distance))
 
     def _scatter(self, part, stage, distance):
         s = self.s
-        src = (s.grads, s.sum1, s.sum2)[stage].at[part, :, self._place(part, stage, distance)]
+        src = s.grads.at[(part, slice(None), *self._mine(part, stage), self._place(part, stage, distance))]
         dst = (s.part0, s.part1, s.part2)[stage].at[part, distance - 1]
         return self._remote(src, dst, part, stage, stage, distance)
 
@@ -571,114 +643,126 @@
         place = self._full(part, *[self._place(part, before) for before in range(stage + 1)])
         return self._remote(place, place, part, stage, 3 + stage, distance)
 
-    def _wait(self, row, part=None):
-        s = self.s
-        place = (s.part0, s.part1, s.part2, s.part0, s.part1, s.part2, None, None, None, s.hop, s.hop)[row]
-        sems = s.sems.at[row]
-        if part is None:
-            remote(place, place, sems.at[3], sems.at[0], self.at.partner()).wait_send()
+    def _whole(self, row):
+        s, sems, every = self.s, self.s.sems, slice(None)
+        if row in (0, 1, 2, HOP):
+            place = s.hop if row == HOP else (s.part0, s.part1, s.part2)[row]
         else:
-            remote(place.at[part], place.at[part], sems.at[3], sems.at[part], self.at.partner()).wait_recv()
-
-    def _begin(self, copies, row, part):
+            three = pl.ds(0, 3)
+            places = {
+                3: (pl.ds(0, 2) if self.ring else three,), 4: (0, three), 5: (0, 0, three), 6: (), BACK: (0,),
+            }[row]
+            place = self._full(every, *places)
+        return remote(place, place, sems.at[row, 0], sems.at[row, 1], self.at.partner())
+
+    def _begin(self, copies, row):
         for copy in copies:
             copy.start()
-        self.at.coming[(self.kind, row, part)] = lambda: self._wait(row, part)
-        if part == 2:
-            self.at.sending.append(lambda: self._wait(row))
-
-    def _arrive(self, row, part):
-        self.at.coming.pop((self.kind, row, part))()
-
-    def _direct(self, make, part, stage, row):
-        self._begin([make(part, stage, distance) for distance in (1, 3, 2)], row, part)
+        self.at.coming[(self.kind, row)] = lambda: self._whole(row).wait_recv()
+        self.at.sending.append(lambda: self._whole(row).wait_send())
+
+    def _arrive(self, row):
+        self.at.coming.pop((self.kind, row))()
+
+    def _direct(self, make, stage, row):
+        self._begin([make(part, stage, distance) for part in range(3) for distance in (1, 3, 2)], row)
 
     def scatter(self):
         s = self.s
+        if not self.ring:
+            self._direct(self._scatter, 0, 0)
+            return
+        copies = []
         for part in range(3):
-            if not self.ring:
-                self._direct(self._scatter, part, 0, 0)
-                continue
             opposite = s.grads.at[part, :, self._place(part, 0, 2)]
-            copies = [
+            copies += [
                 self._remote(opposite.at[:, pl.ds(2 * way, 2)], s.hop.at[part, way], part, 0, HOP, distance)
                 for way, distance in enumerate((1, 3))
             ]
-            self._begin(copies, HOP, part)
+        self._begin(copies, HOP)
 
     def turn(self):
         s = self.s
+        self._arrive(HOP)
+        copies = []
         for part in range(3):
-            self._arrive(HOP, part)
-            copies = []
             for way, distance in enumerate((1, 3)):
                 place = self._place(part, 0, distance)
                 half = pl.ds(2 * way, 2)
                 total = s.grads[part, :, place, half].astype(F32) + s.hop[part, way].astype(F32)
                 s.grads[part, :, place, half] = total.astype(BF16)
                 copies.append(self._remote(s.grads.at[part, :, place], s.part0.at[part, way], part, 0, 0, distance))
-            self._begin(copies, 0, part)
+        self._begin(copies, 0)
 
     def scattered(self, stage):
         s = self.s
+        self._arrive(stage)
+        got = (s.part0, s.part1, s.part2)[stage]
         for part in range(3):
-            self._arrive(stage, part)
-            src = (s.grads, s.sum1, s.sum2)[stage]
-            got = (s.part0, s.part1, s.part2)[stage]
-            total = src[part, :, self._place(part, stage)].astype(F32)
+            mine = self._mine(part, stage + 1)
+            total = s.grads[(part, slice(None), *mine)].astype(F32)
             for index in range(got.shape[1]):
                 total = total + got[part, index].astype(F32)
             total = total.astype(BF16)
-            if stage == 0:
-                s.sum1[part] = total
-            elif stage == 1:
-                s.sum2[part] = total
+            if stage < 2:
+                s.grads[(part, slice(None), *mine)] = total
             else:
-                places = [self._place(part, before) for before in range(3)]
-                self.result[(self.at.core, part, pl.ds(self.first, self.units), *places)] = total
-            if stage < 2:
-                self._direct(self._scatter, part, stage + 1, stage + 1)
-            else:
-                self._direct(self._gather, part, 2, 5)
-
-    def gathered(self, stage):
+                self.result[(self.at.core, part, pl.ds(self.first, self.units), *mine)] = total
+        if stage < 2:
+            self._direct(self._scatter, stage + 1, stage + 1)
+        elif self.spread:
+            self._direct(self._gather, 2, 5)
+
+    def gathered(self, stage, hold=False):
+        self._arrive(3 + stage)
+        if stage == 2:
+            self._direct(self._gather, 1, 4)
+        elif not hold:
+            self.gather_last()
+
+    def gather_last(self):
+        if self.ring:
+            self.gather_some(0, self.spread)
+        else:
+            self._direct(self._gather, 0, 3)
+            self._pass((0,))
+
+    def gather_some(self, begin, end):
+        copies = []
         for part in range(3):
-            self._arrive(3 + stage, part)
-            if stage == 2:
-                self._direct(self._gather, part, 1, 4)
-            else:
-                if self.ring:
-                    self._begin([self._gather(part, 0, distance) for distance in (1, 3)], 3, part)
-                else:
-                    self._direct(self._gather, part, 0, 3)
-                self._pass(part, (0,))
+            units = pl.ds(self.first + begin, end - begin)
+            place = self.result.at[self.at.core, part, units, self._place(part, 0)]
+            copies += [self._remote(place, place, part, 0, 3, distance) for distance in (1, 3)]
+        if end == self.spread:
+            self._begin(copies, 3)
+            self._pass((0,))
+        else:
+            for copy in copies:
+                copy.start()
 
     def gather_turn(self):
-        s = self.s
+        self._arrive(3)
+        copies = []
         for part in range(3):
-            self._arrive(3, part)
-            copies = []
             for way, distance in enumerate((1, 3)):
                 place = self._full(part, self._place(part, 0, 4 - distance), pl.ds(2 * way, 2))
                 copies.append(self._remote(place, place, part, 0, BACK, distance))
-            self._begin(copies, BACK, part)
-            self._pass(part, (1, 3))
+        self._begin(copies, BACK)
+        self._pass((1, 3))
 
     def gather_done(self):
+        self._arrive(BACK if self.ring else 3)
+        self._pass((2,) if self.ring else (1, 2, 3))
+
+    def _pass(self, distances):
+        sems = self.s.sems
         for part in range(3):
-            self._arrive(BACK if self.ring else 3, part)
-            self._pass(part, (2,) if self.ring else (1, 2, 3))
-
-    def _pass(self, part, distances):
-        send, recv = self.s.sems.at[6, part], self.s.sems.at[7, part]
-        for distance in distances:
-            place = self._full(part, self._place(part, 0, distance))
-            remote(place, place, send, recv, self.at.partner()).start()
+            for distance in distances:
+                place = self._full(part, self._place(part, 0, distance))
+                remote(place, place, sems.at[6, 0], sems.at[6, 1], self.at.partner()).start()
         if 2 in distances:
-            whole = self._full(part)
-            passed = remote(whole, whole, send, recv, self.at.partner())
-            self.at.coming[(self.kind, 6, part)] = passed.wait_recv
-            self.at.sending.append(passed.wait_send)
+            self.at.coming[(self.kind, 6)] = lambda: self._whole(6).wait_recv()
+            self.at.sending.append(lambda: self._whole(6).wait_send())
 
 
 def vmem(**shapes):
@@ -694,10 +778,9 @@
         dm_out=((8, half, 128), BF16), dm_in=((8, half, 128), BF16),
         mix_out=((8, half, 128), BF16), mix_in=((8, half, 128), BF16),
         dq_out=((8, half, 128), BF16), dq_in=((8, half, 128), BF16),
-        dkv_part=((2, 8, rows, 128), BF16), dkv_other=((8, rows, 128), BF16),
-        dkv_out=((8, rows, 128), BF16), dkv_in=((8, rows, 128), BF16),
+        dkv_out=((16 if index else 8, rows, 128), BF16), dkv_in=((2, 8, rows, 128) if index else (8, rows, 128), BF16),
         query=((8, rows, 128), BF16), key=((length, 128), BF16), value=((length, 128), BF16),
-        expo=((rows, sum(COUNTS)) if index == 0 else (8 * rows, length), BF16), part=((8, rows, 128), F32),
+        expo=((rows, sum(COUNTS)) if index == 0 else (8 * rows, length), BF16), part=((8, rows, 128) if index else (rows, 128), F32),
         normal=((2, rows, D), F32), scale=((2, rows, 128), F32),
         dfirst=((rows, D), F32),
         n1=((rows, D), BF16), n2=((rows, D), BF16), mixed=((rows, D), BF16), glow=((rows, D), BF16),
@@ -706,24 +789,23 @@
         n1_in=((rows, D), BF16), n2_in=((rows, D), BF16), mixed_in=((rows, D), BF16), glow_in=((rows, D), BF16),
         act_in=((rows, FF // 2), BF16), dhid_in=((rows, FF // 2), BF16),
         dv1_in=((rows, 256), BF16), dproj_in=((rows, 768), BF16),
-        column=((8, rows, 128), F32), line=((8, length), F32),
+        column=((8, rows, 128) if index else (rows, 128), F32), line=((8, length), F32),
     )
-    if index:
-        shapes.update(vmem(slope=((length, 128), F32)))
-    shapes.update(sems=pltpu.SemaphoreType.DMA((5, 8)))
+    if not index:
+        shapes.update(vmem(dkv_part=((2, 8, rows, 128), BF16), dkv_other=((8, rows, 128), BF16)))
+    shapes.update(sems=pltpu.SemaphoreType.DMA((5, 10)))
     return shapes
 
 
 def total_scratch(units):
     ways = 2 if units > 1 else 3
     shapes = vmem(
-        hop=((3, 2, units, 2, 4, 16, 128), BF16),
-        grads=((3, units, 4, 4, 4, 16, 128), BF16),
-        part0=((3, ways, units, 4, 4, 16, 128), BF16), sum1=((3, units, 4, 4, 16, 128), BF16),
-        part1=((3, 3, units, 4, 16, 128), BF16), sum2=((3, units, 4, 16, 128), BF16),
-        part2=((3, 3, units, 16, 128), BF16),
+        grads=((3, units, 4, 4, 4, 16, 128), BF16), part0=((3, ways, units, 4, 4, 16, 128), BF16),
+        part1=((3, 3, units, 4, 16, 128), BF16), part2=((3, 3, units, 16, 128), BF16),
     )
-    shapes.update(sems=pltpu.SemaphoreType.DMA((11, 4)))
+    if units > 1:
+        shapes.update(vmem(hop=((3, 2, units, 2, 4, 16, 128), BF16)))
+    shapes.update(sems=pltpu.SemaphoreType.DMA((9, 2)))
     return shapes
 
 
@@ -735,12 +817,13 @@
         wup=((2, D, FF), BF16), wdown=((2, FF, D), BF16),
         dkey=((SEQ * LONG, 128), F32), dvalue=((SEQ * LONG, 128), F32),
         second=((4, LONG + 8, 128), F32), share=((4, SHORT + 8, 128), F32),
-        work=((4, LONG, 128), F32), spread=((4, LONG, 128), F32),
-        tail=((4, 8, 128), F32), ahead=((4, 8, 128), F32),
+        work=((4, LONG, 128), F32),
+        ahead=((4, 8, 128), F32), before=((EXTRA, D), BF16),
+        tail_out=((8, EXTRA, 128), BF16), tail_in=((8, EXTRA, 128), BF16),
         output=((LONG, D), BF16), result=((LONG, D), F32),
         gsum=((8, D), F32), gain_in=((4, 4, 8, D), F32), gain_out=((3, 8, D), F32),
     )
-    shapes.update(more=pltpu.SemaphoreType.DMA((41,)))
+    shapes.update(more=pltpu.SemaphoreType.DMA((29,)))
     return shapes
 
 
@@ -770,9 +853,9 @@
     ref = spaces[0]
     more = ref.more
     full, short = Layer(at, ref, spaces[1], 0, LONG), Layer(at, ref, spaces[2], 1, SHORT)
-    for kind in range(3):
+    for kind in range(4):
         spaces[3 + kind].first = sum(UNITS[:kind])
-    early, middle, late = (Total(at, spaces[3 + kind], 20 + kind, sums) for kind in range(3))
+    early, middle, minor, late = (Total(at, spaces[3 + kind], 20 + kind, sums) for kind in range(4))
 
     pairs = [
         (tokens, ref.tokens), (gains, ref.gains), (wqkv.at[0], ref.wqkv.at[0]),
@@ -807,6 +890,9 @@
         for head in range(8):
             full.s.kv_out[head, LONG:] = note.astype(BF16)
         pl.semaphore_wait(barrier, greeted)
+        at.start(
+            remote(ref.tokens.at[pl.ds(LONG - EXTRA, EXTRA)], ref.before, more.at[17], more.at[18], at.along(1)), (3, 0)
+        )
 
     full.project(inputs, ready)
 
@@ -826,7 +912,10 @@
                 else:
                     line = (64.0 * code[4:5] + code[5:6])[:, :SHORT]
                 column = jnp.sum(jnp.where(equal, line, 0.0), 1, keepdims=True)
-                layer.s.column[pair] = jnp.broadcast_to(column, (rows, 128))
+                if layer is full:
+                    layer.s.column[:, pair : pair + 1] = column
+                else:
+                    layer.s.column[pair] = jnp.broadcast_to(column, (rows, 128))
 
     def attention(layer):
         layer.receive_keys()
@@ -836,24 +925,18 @@
         layer.split_heads()
         layer.attend()
         layer.receive(MIX)
+        if layer is full:
+            layer.receive(TAIL)
 
     attention(full)
     loaded(9)
     second = ref.second
-    spill(second, 8, full.feed_forward(inputs))
-
-    def halo():
-        return remote(second.at[:, pl.ds(LONG, 8), :], ref.tail, more.at[17], more.at[18], at.along(1))
-
-    at.start(halo(), (3, 0))
+    at.coming.pop((3, 0))()
+    wide = full.feed_forward(jnp.concatenate([inputs, ref.before[...].astype(F32)], 0))
+    spill(second, 8, wide[:LONG])
+    spill(second, 0, jnp.where(at.seq == 0, 0.0, wide[LONG + EXTRA - 8 :]))
+    full.swap(AHEAD)
     loaded(11)
-    work = ref.work
-    spill(work, 0, ref.cot[...].astype(F32))
-    grad_short = jnp.concatenate(
-        [every_third(work, 0, g) + every_third(work, 1, g) + every_third(work, 2, g) for g in range(GROUPS)], 1
-    )
-    at.finish(halo(), (3, 0))
-    second[:, 0:8, :] = jnp.where(at.seq == 0, 0.0, ref.tail[...])
     pooled = jnp.concatenate(
         [
             (every_third(second, 6, g) + every_third(second, 7, g) + every_third(second, 8, g)) / 3.0
@@ -863,37 +946,44 @@
     )
     short.project(pooled)
     loaded(14)
+    work = ref.work
+    spill(work, 0, ref.cot[...].astype(F32))
+    grad_short = jnp.concatenate(
+        [every_third(work, 0, g) + every_third(work, 1, g) + every_third(work, 2, g) for g in range(GROUPS)], 1
+    )
     attention(short)
     result = short.feed_forward(pooled)
+    short.swap(AHEAD)
 
     def backward(layer, total, grad, between):
         layer.feed_back(grad)
-        layer.swap(SEVEN)
         between(0)
-        layer.swapped(SEVEN)
+        layer.swapped(AHEAD)
+        for which in BEHIND:
+            layer.swapped((which,))
         layer.grads_feed(total)
         between(1)
         layer.receive(DM)
         layer.attend_back(between)
-        layer.merge_start()
-        between(3)
-        layer.merge()
-        layer.send(DKV)
+        if layer is full:
+            layer.merge(0)
+            layer.send_rest(DKV)
+        else:
+            layer.send(DKV)
         between(4)
         layer.receive(DQ)
         layer.receive(DKV)
+        between(6)
         back = layer.project_back()
         layer.swap((7,))
         return back
-
-    spread = ref.spread
 
     def finish_output():
         for group in range(GROUPS):
             at_lanes = slice(128 * group, 128 * group + 128)
             for step in range(3):
-                spread[group, pl.ds(step, SHORT, 3), :] = every_third(second, 8 + step, group) + result[:, at_lanes]
-            ref.output[:, at_lanes] = spread[group].astype(BF16)
+                second[group, pl.ds(8 + step, SHORT, 3), :] = every_third(second, 8 + step, group) + result[:, at_lanes]
+            ref.output[:, at_lanes] = second[group, 8:, :].astype(BF16)
         store = pltpu.make_async_copy(ref.output, output, more.at[14])
         store.start()
         at.sending.append(store.wait)
@@ -901,8 +991,10 @@
     def between_short(point):
         if point == 0:
             finish_output()
+        elif point == 1:
+            early.scatter()
         elif point == 4:
-            early.scatter()
+            early.turn()
 
     share = ref.share
     spill(share, 0, backward(short, early, grad_short, between_short) * (1.0 / 3.0))
@@ -911,37 +1003,43 @@
         return remote(share.at[:, pl.ds(0, 8), :], ref.ahead, more.at[19], more.at[20], at.along(SEQ - 1))
 
     at.start(halo_back(), (3, 1))
-    early.turn()
     short.swapped((7,))
-    short.grads_attention(middle, 9)
+    short.grads_attention(minor, 0)
+    minor.scatter()
     at.finish(halo_back(), (3, 1))
+    early.scattered(0)
     share[:, SHORT:, :] = jnp.where(at.seq == SEQ - 1, 0.0, ref.ahead[...])
     for group in range(GROUPS):
         own, following = share[group, 0:SHORT, :], share[group, 1 : SHORT + 1, :]
         for step, piece in enumerate((own, following, following)):
-            spread[group, pl.ds(step, SHORT, 3), :] = every_third(work, step, group) + piece
-    grad_full = jnp.concatenate([spread[group] for group in range(GROUPS)], 1)
+            work[group, pl.ds(step, SHORT, 3), :] = every_third(work, step, group) + piece
+    grad_full = jnp.concatenate([work[group] for group in range(GROUPS)], 1)
 
     def between_full(point):
-        if point == 0:
-            early.scattered(0)
-        elif point == 1:
+        if point == 1:
             middle.scatter()
             early.scattered(1)
-        elif point == 2:
+        elif point == 17:
+            minor.scattered(0)
+        elif point == 16:
             early.scattered(2)
+        elif point == 15:
             middle.turn()
-        elif point == 3:
+        elif point == 13:
             early.gathered(2)
-        else:
+        elif point == 11:
+            minor.scattered(1)
+        elif point == 4:
             middle.scattered(0)
             early.gathered(1)
+            minor.scattered(2)
+        elif point == 6:
+            middle.scattered(1)
 
     ref.result[...] = backward(full, middle, grad_full, between_full)
     store = pltpu.make_async_copy(ref.result, tokens_grad, more.at[15])
     store.start()
     at.sending.append(store.wait)
-    middle.scattered(1)
     full.swapped((7,))
     full.grads_attention(late, 0)
     late.scatter()
@@ -950,25 +1048,25 @@
 
     def gain_copy(axis, distance):
         src = gsum if axis == 0 else gain_out.at[axis - 1]
-        return remote(
-            src, gain_in.at[axis, at.at[axis]], more.at[22 + 3 * axis + distance], more.at[31 + 3 * axis + distance],
-            at.peer(axis, distance),
-        )
+        return remote(src, gain_in.at[axis, at.at[axis]], more.at[23 + axis], more.at[26 + axis], at.peer(axis, distance))
 
     def gain_step(axis):
         for distance in (1, 2, 3):
-            at.start(gain_copy(axis, distance), (4, axis, distance))
+            gain_copy(axis, distance).start()
         gain_in[axis, at.at[axis]] = gsum[...] if axis == 0 else gain_out[axis - 1]
+        three = gain_in.at[axis, pl.ds(0, 3)]
+        copies = remote(three, three, more.at[23 + axis], more.at[26 + axis], at.partner())
+        at.coming[(4, axis)] = copies.wait_recv
+        at.sending.append(copies.wait_send)
 
     def gain_done(axis):
-        for distance in (1, 2, 3):
-            at.finish(gain_copy(axis, distance), (4, axis, distance))
+        at.coming.pop((4, axis))()
         return (gain_in[axis, 0] + gain_in[axis, 1]) + (gain_in[axis, 2] + gain_in[axis, 3])
 
     gsum[4:, :] = jnp.zeros((4, D), F32)
     gain_step(0)
+    middle.scattered(2)
     early.gather_turn()
-    middle.scattered(2)
     late.scattered(0)
     gain_out[0] = gain_done(0)
     gain_step(1)
@@ -976,17 +1074,19 @@
     late.scattered(1)
     gain_out[1] = gain_done(1)
     gain_step(2)
+    late.scattered(2)
+    middle.gathered(1, True)
+    middle.gather_some(0, 2)
     early.gather_done()
-    late.scattered(2)
-    middle.gathered(1)
     late.gathered(2)
+    middle.gather_some(2, 4)
+    late.gathered(1)
     middle.gather_turn()
-    late.gathered(1)
     gain_in[3, 0] = gain_done(2)
     gain_swap = remote(gain_in.at[3, 0], gain_in.at[3, 1], more.at[21], more.at[22], at.partner())
     at.start(gain_swap, (4, 3, 0))
+    late.gather_done()
     middle.gather_done()
-    late.gather_done()
     at.finish(gain_swap, (4, 3, 0))
     gain_out[2] = gain_in[3, 0] + gain_in[3, 1]
     store = pltpu.make_async_copy(gain_out.at[2], gain_sum, more.at[16])
@@ -1065,7 +1165,7 @@
         put(output_too.at[0], output_in, 11)
         put(grad_too.at[0], grad_in, 12)
 
-    for kind, block, kind_heads, unit in ((0, 1, 1, 9), (1, 0, 2, 0)):
+    for kind, block, kind_heads, unit in ((0, 1, 2, 0), (1, 0, 3, 0)):
         for half in range(2):
             feed(kind, half, block)
         rest(kind, block, kind_heads, unit)

time: 144 us -> 140 us (0.972)
  Pallas kernels: 143 us -> 139 us
    pallas_call x1, Pallas kernels: 134 us -> 130 us  [per_device(): pl.pallas_call(body, out_shape=(jax.ShapeDtypeStruct((LONG, D), BF16), ja...]
where the time goes in v3:
time: 140 us; the launch traced here: 139 us
  Pallas kernels  139 us (99%)
    pallas_call x1, Pallas kernels, per_device(): pl.pallas_call(body, out_shape=(jax.ShapeDtypeStruct((LONG, D), BF16), ja...  130 us
    pallas_call x1, Pallas kernels, widen(): pl.pallas_call(widen_body, out_shape=(jax.ShapeDtypeStruct((2, D, 3 * D),...  9 us

profile of v3, /device:TPU:1, one launch (start us, length us, event | category | flops | bytes accessed | tf_op | source)
XLA Modules:
  0.0 139.5 jit_solution(14692604222088471331)
XLA Ops:
  0.6 129.6 %layers.1 = (bf16[144,512]{1,0:T(8,128)(2,1)}, f32[144,512]{1,0:T(8,128)}, bf16[2,3,8,4,4,4,16,128]{7,6,5,4,3,2,1,0:T(8,128)(2,1)S(1)}, f32[8,512]{1,0:T(8,128)}) custom-call(bf16[144,512]{1,0:T(8,128)(2,1)} %bitcast.2, s32[1,144]{1,0:T(1,128)} %refs_1_.1, bf16[2,512,1536]{2,1,0:T(8,128)(2,1)} %refs_2_.1, bf16[2,512,512]{2,1,0:T(8,128)(2,1)} %refs_3_.1, ...), custom_call_target="tpu_custom_call" | custom-call | tf_op jit(solution)/shard_map/layers/pallas_call | solution.py:1215
  130.3 9.0 %widen.1 = (f32[2,512,1536]{2,1,0:T(8,128)}, f32[2,512,512]{2,1,0:T(8,128)}, f32[2,512,2048]{2,1,0:T(8,128)}, f32[2,2048,512]{2,1,0:T(8,128)}, f32[2,2,512]{2,1,...) custom-call(bf16[2,3,8,4,4,4,16,128]{7,6,5,4,3,2,1,0:T(8,128)(2,1)S(1)} %get-tuple-element.18.sums, ...), custom_call_target="tpu_custom_call" | custom-call | tf_op jit(solution)/shard_map/widen/pallas_call | solution.py:1180

commit v4 on v3

--- a/solution.py
+++ b/solution.py
@@ -186,6 +186,10 @@
         self.rows = rows
         self.slope = ref.dvalue if index else ref.dkey
 
+    def _sem(self, row, column):
+        rows = (0, 10, 20, 28, 36) if self.index == 0 else (0, 6, None, 12, 20)
+        return self.s.sems.at[rows[row] + column]
+
 
     def _buffers(self, kind):
         s = self.s
@@ -198,9 +202,9 @@
         return self.index == 1 and kind in (KV, DKV)
 
     def _copy(self, kind, index):
-        at, sems = self.at, self.s.sems
+        at = self.at
         out, into = self._buffers(kind)
-        source, recv = index, sems.at[1, kind]
+        source, recv = index, self._sem(1, kind)
         if kind in (KV, Q, DM):
             if self._wide(kind):
                 source = index // 2
@@ -209,7 +213,7 @@
                 device, same = at.holder(index, lax.rem(at.seq, 2))
             target = at.seq if kind == KV else at.seq // 2
             if kind == KV and not self._wide(kind):
-                recv = sems.at[2, at.seq // 2]
+                recv = self._sem(2, at.seq // 2)
             into = into.at[target]
         elif self._wide(kind):
             device, same = at.owner(index)
@@ -217,7 +221,7 @@
         else:
             device, same = at.owner(lax.rem(2 * index + at.core + (1 if kind == TAIL else 0), SEQ))
             into = into.at[at.head]
-        return out.at[source], into, sems.at[0, kind], recv, device, same
+        return out.at[source], into, self._sem(0, kind), recv, device, same
 
     def send_one(self, kind, index):
         src, dst, send, recv, device, same = self._copy(kind, index)
@@ -261,11 +265,9 @@
 
     def receive(self, kind):
         self.at.coming.pop((self.index, kind), None)
-        sems = self.s.sems
-        self._wait(self._buffers(kind)[1], sems.at[0, kind], sems.at[1, kind]).wait_recv()
+        self._wait(self._buffers(kind)[1], self._sem(0, kind), self._sem(1, kind)).wait_recv()
 
     def sent(self, kind):
-        sems = self.s.sems
         count = 16 if self._wide(kind) else 8
         many = self.s.kv_in if kind == KV else self._buffers(kind)[0]
         inside = self.at.near if self._wide(kind) else self.at.next if kind == TAIL else self.at.same
@@ -273,12 +275,11 @@
 
             @pl.when(when)
             def _():
-                self._wait(many.at[pl.ds(0, number)], sems.at[0, kind], sems.at[1, kind]).wait_send()
+                self._wait(many.at[pl.ds(0, number)], self._sem(0, kind), self._sem(1, kind)).wait_send()
 
     def _relay(self, index):
         place = self.s.kv_in.at[2 * index + self.at.core]
-        sems = self.s.sems
-        return remote(place, place, sems.at[0, RELAY], sems.at[1, RELAY], self.at.partner())
+        return remote(place, place, self._sem(0, RELAY), self._sem(1, RELAY), self.at.partner())
 
     def receive_keys(self):
         if self._wide(KV):
@@ -288,12 +289,12 @@
         s = self.s
 
         def one(index, carry):
-            self._wait(s.kv_in.at[0], s.sems.at[0, KV], s.sems.at[2, index]).wait_recv()
+            self._wait(s.kv_in.at[0], self._sem(0, KV), self._sem(2, index)).wait_recv()
             self._relay(index).start()
             return carry
 
         lax.fori_loop(0, 8, one, 0)
-        relayed = self._wait(s.kv_in.at[pl.ds(0, 8)], s.sems.at[0, RELAY], s.sems.at[1, RELAY])
+        relayed = self._wait(s.kv_in.at[pl.ds(0, 8)], self._sem(0, RELAY), self._sem(1, RELAY))
         relayed.wait_recv()
         self.at.sending.append(relayed.wait_send)
 
@@ -520,7 +521,7 @@
 
     def _merge(self, half):
         s, four = self.s, pl.ds(4 * half, 4)
-        send, recv = s.sems.at[0, MERGE + half], s.sems.at[1, MERGE + half]
+        send, recv = self._sem(0, MERGE + half), self._sem(1, MERGE + half)
         return remote(s.dkv_part.at[1 - self.at.core, four], s.dkv_other.at[four], send, recv, self.at.partner())
 
     def merge(self, half):
@@ -564,7 +565,7 @@
             (s.glow, s.glow_in), (s.n2, s.n2_in), (s.act.at[other], s.act_in), (s.dhid.at[other], s.dhid_in),
             (s.mixed, s.mixed_in), (s.dv1.at[other], s.dv1_in), (s.n1, s.n1_in), (s.dproj.at[other], s.dproj_in),
         )[which]
-        return remote(src, dst, s.sems.at[3, which], s.sems.at[4, which], self.at.partner())
+        return remote(src, dst, self._sem(3, which), self._sem(4, which), self.at.partner())
 
     def swap(self, steps):
         copies = [self._swap(which) for which in steps]
@@ -793,11 +794,11 @@
     )
     if not index:
         shapes.update(vmem(dkv_part=((2, 8, rows, 128), BF16), dkv_other=((8, rows, 128), BF16)))
-    shapes.update(sems=pltpu.SemaphoreType.DMA((5, 10)))
+    shapes.update(sems=pltpu.SemaphoreType.DMA((28 if index else 44,)))
     return shapes
 
 
-def total_scratch(units):
+def total_scratch(units, rows):
     ways = 2 if units > 1 else 3
     shapes = vmem(
         grads=((3, units, 4, 4, 4, 16, 128), BF16), part0=((3, ways, units, 4, 4, 16, 128), BF16),
@@ -805,7 +806,7 @@
     )
     if units > 1:
         shapes.update(vmem(hop=((3, 2, units, 2, 4, 16, 128), BF16)))
-    shapes.update(sems=pltpu.SemaphoreType.DMA((9, 2)))
+    shapes.update(sems=pltpu.SemaphoreType.DMA((rows, 2)))
     return shapes
 
 
@@ -829,7 +830,7 @@
 
 SPACES = (
     common_scratch(), layer_scratch(0, LONG), layer_scratch(1, SHORT),
-    *(total_scratch(units) for units in UNITS),
+    *(total_scratch(units, rows) for units, rows in zip(UNITS, (9, 9, 3, 7))),
 )
 
 
@@ -919,10 +920,10 @@
 
     def attention(layer):
         layer.receive_keys()
-        layer.receive(Q)
         if layer is full:
             segments()
         layer.split_heads()
+        layer.receive(Q)
         layer.attend()
         layer.receive(MIX)
         if layer is full:
@@ -1005,9 +1006,7 @@
     at.start(halo_back(), (3, 1))
     short.swapped((7,))
     short.grads_attention(minor, 0)
-    minor.scatter()
     at.finish(halo_back(), (3, 1))
-    early.scattered(0)
     share[:, SHORT:, :] = jnp.where(at.seq == SEQ - 1, 0.0, ref.ahead[...])
     for group in range(GROUPS):
         own, following = share[group, 0:SHORT, :], share[group, 1 : SHORT + 1, :]
@@ -1016,25 +1015,23 @@
     grad_full = jnp.concatenate([work[group] for group in range(GROUPS)], 1)
 
     def between_full(point):
-        if point == 1:
+        if point == 0:
+            early.scattered(0)
+        elif point == 1:
             middle.scatter()
+            minor.scatter()
+        elif point == 17:
             early.scattered(1)
-        elif point == 17:
-            minor.scattered(0)
-        elif point == 16:
-            early.scattered(2)
-        elif point == 15:
+        elif point == 14:
             middle.turn()
         elif point == 13:
-            early.gathered(2)
+            early.scattered(2)
         elif point == 11:
-            minor.scattered(1)
+            minor.scattered(0)
         elif point == 4:
             middle.scattered(0)
-            early.gathered(1)
-            minor.scattered(2)
-        elif point == 6:
-            middle.scattered(1)
+            early.gathered(2)
+            minor.scattered(1)
 
     ref.result[...] = backward(full, middle, grad_full, between_full)
     store = pltpu.make_async_copy(ref.result, tokens_grad, more.at[15])
@@ -1043,7 +1040,6 @@
     full.swapped((7,))
     full.grads_attention(late, 0)
     late.scatter()
-
     gsum, gain_in, gain_out = ref.gsum, ref.gain_in, ref.gain_out
 
     def gain_copy(axis, distance):
@@ -1065,22 +1061,25 @@
 
     gsum[4:, :] = jnp.zeros((4, D), F32)
     gain_step(0)
+    middle.scattered(1)
+    minor.scattered(2)
+    early.gathered(1)
+    late.scattered(0)
     middle.scattered(2)
-    early.gather_turn()
-    late.scattered(0)
+    late.scattered(1)
+    middle.gathered(2)
     gain_out[0] = gain_done(0)
     gain_step(1)
-    middle.gathered(2)
-    late.scattered(1)
+    late.scattered(2)
+    early.gather_turn()
+    middle.gathered(1, True)
+    middle.gather_some(0, 2)
+    late.gathered(2)
     gain_out[1] = gain_done(1)
     gain_step(2)
-    late.scattered(2)
-    middle.gathered(1, True)
-    middle.gather_some(0, 2)
-    early.gather_done()
-    late.gathered(2)
     middle.gather_some(2, 4)
     late.gathered(1)
+    early.gather_done()
     middle.gather_turn()
     gain_in[3, 0] = gain_done(2)
     gain_swap = remote(gain_in.at[3, 0], gain_in.at[3, 1], more.at[21], more.at[22], at.partner())

time: 140 us -> 140 us (level)
  no operation moved by 1% of the time
where the time goes in v4:
time: 140 us
  Pallas kernels  139 us (99%)
    pallas_call x1, Pallas kernels, per_device(): pl.pallas_call(body, out_shape=(jax.ShapeDtypeStruct((LONG, D), BF16), ja...  130 us
    pallas_call x1, Pallas kernels, widen(): pl.pallas_call(widen_body, out_shape=(jax.ShapeDtypeStruct((2, D, 3 * D),...  9 us

profile of v4, /device:TPU:1, one launch (start us, length us, event | category | flops | bytes accessed | tf_op | source)
XLA Modules:
  0.0 139.8 jit_solution(4985479467158718113)
XLA Ops:
  0.6 130.0 %layers.1 = (bf16[144,512]{1,0:T(8,128)(2,1)}, f32[144,512]{1,0:T(8,128)}, bf16[2,3,8,4,4,4,16,128]{7,6,5,4,3,2,1,0:T(8,128)(2,1)S(1)}, f32[8,512]{1,0:T(8,128)}) custom-call(bf16[144,512]{1,0:T(8,128)(2,1)} %bitcast.2, s32[1,144]{1,0:T(1,128)} %refs_1_.1, bf16[2,512,1536]{2,1,0:T(8,128)(2,1)} %refs_2_.1, bf16[2,512,512]{2,1,0:T(8,128)(2,1)} %refs_3_.1, ...), custom_call_target="tpu_custom_call" | custom-call | tf_op jit(solution)/shard_map/layers/pallas_call | solution.py:1214
  130.6 9.0 %widen.1 = (f32[2,512,1536]{2,1,0:T(8,128)}, f32[2,512,512]{2,1,0:T(8,128)}, f32[2,512,2048]{2,1,0:T(8,128)}, f32[2,2048,512]{2,1,0:T(8,128)}, f32[2,2,512]{2,1,...) custom-call(bf16[2,3,8,4,4,4,16,128]{7,6,5,4,3,2,1,0:T(8,128)(2,1)S(1)} %get-tuple-element.18.sums, ...), custom_call_target="tpu_custom_call" | custom-call | tf_op jit(solution)/shard_map/widen/pallas_call | solution.py:1179

commit v5 on v4

--- a/solution.py
+++ b/solution.py
@@ -817,8 +817,8 @@
         wqkv=((2, D, 3 * D), BF16), wout=((2, D, D), BF16),
         wup=((2, D, FF), BF16), wdown=((2, FF, D), BF16),
         dkey=((SEQ * LONG, 128), F32), dvalue=((SEQ * LONG, 128), F32),
-        second=((4, LONG + 8, 128), F32), share=((4, SHORT + 8, 128), F32),
-        work=((4, LONG, 128), F32),
+        second=((4, LONG + 16, 128), F32), share=((4, SHORT + 8, 128), F32),
+        work=((4, LONG + 8, 128), F32),
         ahead=((4, 8, 128), F32), before=((EXTRA, D), BF16),
         tail_out=((8, EXTRA, 128), BF16), tail_in=((8, EXTRA, 128), BF16),
         output=((LONG, D), BF16), result=((LONG, D), F32),
@@ -984,7 +984,7 @@
             at_lanes = slice(128 * group, 128 * group + 128)
             for step in range(3):
                 second[group, pl.ds(8 + step, SHORT, 3), :] = every_third(second, 8 + step, group) + result[:, at_lanes]
-            ref.output[:, at_lanes] = second[group, 8:, :].astype(BF16)
+            ref.output[:, at_lanes] = second[group, 8 : 8 + LONG, :].astype(BF16)
         store = pltpu.make_async_copy(ref.output, output, more.at[14])
         store.start()
         at.sending.append(store.wait)
@@ -1012,7 +1012,7 @@
         own, following = share[group, 0:SHORT, :], share[group, 1 : SHORT + 1, :]
         for step, piece in enumerate((own, following, following)):
             work[group, pl.ds(step, SHORT, 3), :] = every_third(work, step, group) + piece
-    grad_full = jnp.concatenate([work[group] for group in range(GROUPS)], 1)
+    grad_full = jnp.concatenate([work[group, :LONG, :] for group in range(GROUPS)], 1)
 
     def between_full(point):
         if point == 0:

time: 140 us -> 140 us (level)
  no operation moved by 1% of the time
where the time goes in v5:
time: 140 us
  Pallas kernels  139 us (99%)
    pallas_call x1, Pallas kernels, per_device(): pl.pallas_call(body, out_shape=(jax.ShapeDtypeStruct((LONG, D), BF16), ja...  130 us
    pallas_call x1, Pallas kernels, widen(): pl.pallas_call(widen_body, out_shape=(jax.ShapeDtypeStruct((2, D, 3 * D),...  9 us

profile of v5, /device:TPU:1, one launch (start us, length us, event | category | flops | bytes accessed | tf_op | source)
XLA Modules:
  0.0 139.8 jit_solution(10500749375327342631)
XLA Ops:
  0.6 130.0 %layers.1 = (bf16[144,512]{1,0:T(8,128)(2,1)}, f32[144,512]{1,0:T(8,128)}, bf16[2,3,8,4,4,4,16,128]{7,6,5,4,3,2,1,0:T(8,128)(2,1)S(1)}, f32[8,512]{1,0:T(8,128)}) custom-call(bf16[144,512]{1,0:T(8,128)(2,1)} %bitcast.2, s32[1,144]{1,0:T(1,128)} %refs_1_.1, bf16[2,512,1536]{2,1,0:T(8,128)(2,1)} %refs_2_.1, bf16[2,512,512]{2,1,0:T(8,128)(2,1)} %refs_3_.1, ...), custom_call_target="tpu_custom_call" | custom-call | tf_op jit(solution)/shard_map/layers/pallas_call | solution.py:1214
  130.7 9.0 %widen.1 = (f32[2,512,1536]{2,1,0:T(8,128)}, f32[2,512,512]{2,1,0:T(8,128)}, f32[2,512,2048]{2,1,0:T(8,128)}, f32[2,2048,512]{2,1,0:T(8,128)}, f32[2,2,512]{2,1,...) custom-call(bf16[2,3,8,4,4,4,16,128]{7,6,5,4,3,2,1,0:T(8,128)(2,1)S(1)} %get-tuple-element.18.sums, ...), custom_call_target="tpu_custom_call" | custom-call | tf_op jit(solution)/shard_map/widen/pallas_call | solution.py:1179
